TPU v7x, 256 devices: a whole 4x4x8 slice. The times are simulated.
256 devices in a mesh: cell: 128 (over z, x, y), view: 2 (over core).
Axes of the slice: x: 4, y: 4, z: 8, core: 2. Of those that a mesh axis runs over, the one named last changes fastest.
Arguments:
- gauss_params: float32 [59, 4915200], P(None, ('cell', 'view')), as said below
- visible: int32 [4, 4915200], P(None, ('cell', 'view')), may hold values 0 or 1
- cameras: float32 [4, 15], replicated, as said below
- tile_ids: int32 [128, 2, 120], P('cell', 'view'), may hold values from 0 to 15359, as said below
- tile_blocks: int32 [128, 2, 120, 2], P('cell', 'view'), may hold values from -1 to 38399, as said below
- target: float32 [2, 3, 2048, 1920], P('view', None, 'cell'), as said below
Outputs:
- image: float32 [2, 3, 2048, 1920], P('view', None, 'cell')
- loss_map: float32 [2, 2048, 1920], P('view', 'cell')
Inputs may be any that keep to these rules, and one draw needn't show every extreme that they name: `tile_ids`: for each view index v the lists of the 128 renderers (c, v) together name each of the 15360 tiles of views 2 v and 2 v + 1 exactly once. The tiles of one renderer lie in 120 different columns t % 120, at most 1 of them in one stripe t // 120, and some renderer reaches 1. `tile_blocks`: an entry names a block g (Gaussians 128 g to 128 g + 127, held by device g // 150 of cell+view) or is -1. The live entries of a tile come first, 1 to 2 of them, and some tile has 2. Every block is named by exactly one tile of all. The live entries of one renderer number exactly 150; at most 1 of them name blocks of one device, and every renderer reaches 1 with some device. `gauss_params`: rows 0 to 2: mean; 3 to 5: logarithms of the scales; 6 to 9: rotation quaternion, real part in row 6 between 1 and 2; row 10: opacity logit, at most 2; row 11 + 3 j + k: coefficient j of the spherical harmonics of colour channel k. Every Gaussian of a block named by a tile lies at depth about 4 to 40 in front of the camera of that tile's view. `cameras`: row w: a rotation (world to camera, row-major) in entries 0 to 8, the translation in 9 to 11, the focal length in pixels in 12 and the principal point (column, row) in 13 and 14. `target`: every value lies between 0.02 and 1.
All inputs are finite; a program needn't handle non-finite values. No bound on the sum of `visible` on one device may be relied on, other than what follows from the above.
Results may differ from a plain program's by a relative error of at most 0.0003.
Values sent between devices are 32-bit elements; how exact they have to be, the bound alone decides.
A program may use at most 64 MiB of HBM per device.

v0:
```python
import jax
import jax.numpy as jnp
from jax import lax
from jax.sharding import PartitionSpec as P

GBLK = 128


def with_halo(cells, sides, width):
    for axis, dim in sides:
        count = lax.axis_size(axis)
        head = lax.slice_in_dim(cells, 0, width, axis=dim)
        tail = lax.slice_in_dim(cells, cells.shape[dim] - width, cells.shape[dim], axis=dim)
        cells = jnp.concatenate(
            [
                lax.ppermute(tail, axis, [(i, (i + 1) % count) for i in range(count)]),
                cells,
                lax.ppermute(head, axis, [((i + 1) % count, i) for i in range(count)]),
            ],
            axis=dim,
        )
    return cells


def harmonics(unit_x, unit_y, unit_z):
    square_x = unit_x * unit_x
    square_y = unit_y * unit_y
    square_z = unit_z * unit_z
    return [
        0.28209479177387814 + 0.0 * unit_x,
        -0.4886025119029199 * unit_y,
        0.4886025119029199 * unit_z,
        -0.4886025119029199 * unit_x,
        1.0925484305920792 * unit_x * unit_y,
        -1.0925484305920792 * unit_y * unit_z,
        0.31539156525252005 * (2.0 * square_z - square_x - square_y),
        -1.0925484305920792 * unit_x * unit_z,
        0.5462742152960396 * (square_x - square_y),
        -0.5900435899266435 * unit_y * (3.0 * square_x - square_y),
        2.890611442640554 * unit_x * unit_y * unit_z,
        -0.4570457994644658 * unit_y * (4.0 * square_z - square_x - square_y),
        0.3731763325901154 * unit_z * (2.0 * square_z - 3.0 * square_x - 3.0 * square_y),
        -0.4570457994644658 * unit_x * (4.0 * square_z - square_x - square_y),
        1.445305721320277 * unit_z * (square_x - square_y),
        -0.5900435899266435 * unit_x * (square_x - 3.0 * square_y),
    ]


def project(raw_params, camera, seen_mask):
    entries = [camera[:, number][:, None] for number in range(15)]
    rotation = [
        [entries[0], entries[1], entries[2]],
        [entries[3], entries[4], entries[5]],
        [entries[6], entries[7], entries[8]],
    ]
    offset = [entries[9], entries[10], entries[11]]
    focal_len = entries[12]
    centre_pos = [raw_params[:, number] for number in range(3)]
    in_camera = [
        rotation[member][0] * centre_pos[0]
        + rotation[member][1] * centre_pos[1]
        + rotation[member][2] * centre_pos[2]
        + offset[member]
        for member in range(3)
    ]
    depths = in_camera[2]
    screen_x = focal_len * in_camera[0] / depths + entries[13]
    screen_y = focal_len * in_camera[1] / depths + entries[14]
    quaternion = [raw_params[:, 6 + number] for number in range(4)]
    length = jnp.sqrt(
        quaternion[0] * quaternion[0]
        + quaternion[1] * quaternion[1]
        + quaternion[2] * quaternion[2]
        + quaternion[3] * quaternion[3]
    )
    real_part, imag_x, imag_y, imag_z = [part / length for part in quaternion]
    turn_q = [
        [
            1.0 - 2.0 * (imag_y * imag_y + imag_z * imag_z),
            2.0 * (imag_x * imag_y - real_part * imag_z),
            2.0 * (imag_x * imag_z + real_part * imag_y),
        ],
        [
            2.0 * (imag_x * imag_y + real_part * imag_z),
            1.0 - 2.0 * (imag_x * imag_x + imag_z * imag_z),
            2.0 * (imag_y * imag_z - real_part * imag_x),
        ],
        [
            2.0 * (imag_x * imag_z - real_part * imag_y),
            2.0 * (imag_y * imag_z + real_part * imag_x),
            1.0 - 2.0 * (imag_x * imag_x + imag_y * imag_y),
        ],
    ]
    squares = [jnp.exp(2.0 * raw_params[:, 3 + number]) for number in range(3)]
    jacobian = [
        [focal_len / depths, 0.0 * depths, -focal_len * in_camera[0] / (depths * depths)],
        [0.0 * depths, focal_len / depths, -focal_len * in_camera[1] / (depths * depths)],
    ]
    with_cam = [
        [
            jacobian[member][0] * rotation[0][column]
            + jacobian[member][1] * rotation[1][column]
            + jacobian[member][2] * rotation[2][column]
            for column in range(3)
        ]
        for member in range(2)
    ]
    whole = [
        [
            with_cam[member][0] * turn_q[0][column]
            + with_cam[member][1] * turn_q[1][column]
            + with_cam[member][2] * turn_q[2][column]
            for column in range(3)
        ]
        for member in range(2)
    ]
    cov_a = (
        squares[0] * whole[0][0] * whole[0][0]
        + squares[1] * whole[0][1] * whole[0][1]
        + squares[2] * whole[0][2] * whole[0][2]
        + 0.3
    )
    cov_b = (
        squares[0] * whole[0][0] * whole[1][0]
        + squares[1] * whole[0][1] * whole[1][1]
        + squares[2] * whole[0][2] * whole[1][2]
    )
    cov_c = (
        squares[0] * whole[1][0] * whole[1][0]
        + squares[1] * whole[1][1] * whole[1][1]
        + squares[2] * whole[1][2] * whole[1][2]
        + 0.3
    )
    determinant = cov_a * cov_c - cov_b * cov_b
    eye_pos = [
        -(
            rotation[0][column] * offset[0]
            + rotation[1][column] * offset[1]
            + rotation[2][column] * offset[2]
        )
        for column in range(3)
    ]
    heading = [centre_pos[column] - eye_pos[column] for column in range(3)]
    distance = jnp.sqrt(heading[0] * heading[0] + heading[1] * heading[1] + heading[2] * heading[2])
    basis = harmonics(heading[0] / distance, heading[1] / distance, heading[2] / distance)
    colours = [
        jnp.maximum(
            0.5
            + sum(
                (basis[number] * raw_params[:, 11 + 3 * number + channel] for number in range(16))
            ),
            0.0,
        )
        for channel in range(3)
    ]
    opacity = seen_mask / (1.0 + jnp.exp(-raw_params[:, 10]))
    return jnp.stack(
        [
            screen_x,
            screen_y,
            cov_c / determinant,
            -cov_b / determinant,
            cov_a / determinant,
            opacity,
        ]
        + colours,
        axis=1,
    )


def opacity_terms(features, across_x, across_y):
    dist_x = across_x[:, :, None] - features[:, 0][:, None, :]
    dist_y = across_y[:, :, None] - features[:, 1][:, None, :]
    exponent = (
        -0.5
        * (
            features[:, 2][:, None, :] * dist_x * dist_x
            + features[:, 4][:, None, :] * dist_y * dist_y
        )
        - features[:, 3][:, None, :] * dist_x * dist_y
    )
    alphas = features[:, 5][:, None, :] * jnp.exp(exponent)
    return (alphas, jnp.log1p(-alphas))


def before_sums(log_keep, upper):
    return jnp.einsum("tpg,gh->tph", log_keep, upper, precision=lax.Precision.HIGHEST)


def blend_slot(features, across_x, across_y, log_trans, colour, upper):
    alphas, log_keep = opacity_terms(features, across_x, across_y)
    weights = alphas * jnp.exp(log_trans[:, :, None] + before_sums(log_keep, upper))
    colour = colour + jnp.einsum(
        "tpg,tcg->tcp", weights, features[:, 6:9], precision=lax.Precision.HIGHEST
    )
    return (log_trans + jnp.sum(log_keep, axis=2), colour)


def request_lookup(codes, source_group, gauss_params, visible, cameras):
    blocks = gauss_params.shape[1] // GBLK
    is_live = codes >= 0
    clipped = jnp.maximum(codes, 0)
    local_slot = clipped % blocks
    view_ids = 2 * source_group + clipped // blocks
    raw_params = jnp.moveaxis(
        gauss_params.reshape(gauss_params.shape[0], blocks, GBLK)[:, local_slot], 0, 1
    )
    seen_mask = (
        visible.reshape(visible.shape[0], blocks, GBLK)[view_ids, local_slot].astype(jnp.float32)
        * is_live.astype(jnp.float32)[:, None]
    )
    chooser = (view_ids[:, None] == jnp.arange(cameras.shape[0], dtype=jnp.int32)[None, :]).astype(
        jnp.float32
    )
    camera = jnp.sum(chooser[:, :, None] * cameras[None, :, :], axis=1)
    return project(raw_params, camera, seen_mask)


def window_taps():
    offsets = jnp.arange(11).astype(jnp.float32) - 5.0
    taps = jnp.exp(-offsets * offsets / 4.5)
    return taps / jnp.sum(taps)


def blur(stack, row_count):
    taps = window_taps()
    columns = stack.shape[-1]
    widths = [(0, 0)] * (stack.ndim - 1) + [(5, 5)]
    wide = jnp.pad(stack, widths)
    across = sum((taps[number] * wide[..., number : number + columns] for number in range(11)))
    return sum((taps[number] * across[..., number : number + row_count, :] for number in range(11)))


def stripe_loss(images, targets, row_count):
    stack = jnp.stack([images, targets, images * images, targets * targets, images * targets])
    blurred = blur(stack, row_count)
    mean_x = blurred[0]
    mean_y = blurred[1]
    var_x = blurred[2] - mean_x * mean_x
    var_y = blurred[3] - mean_y * mean_y
    covar = blurred[4] - mean_x * mean_y
    ssim_map = (
        (2.0 * mean_x * mean_y + 0.0001)
        * (2.0 * covar + 0.0009)
        / ((mean_x * mean_x + mean_y * mean_y + 0.0001) * (var_x + var_y + 0.0009))
    )
    inner_x = images[..., 5 : 5 + row_count, :]
    inner_y = targets[..., 5 : 5 + row_count, :]
    return 0.8 * jnp.mean(jnp.abs(inner_x - inner_y), axis=-3) + 0.2 * (
        1.0 - jnp.mean(ssim_map, axis=-3)
    )


def local(gauss_params, visible, cameras, tile_ids, tile_blocks, target):
    cells = lax.axis_size("cell")
    groups = lax.axis_size("view")
    devices = cells * groups
    half = cells // 2
    quarter = cells // 4
    my_cell = lax.axis_index("cell")
    blocks = gauss_params.shape[1] // GBLK
    capacity = -(-blocks // devices)
    per_row = target.shape[3] // 16
    tile_list = tile_ids[0, 0]
    entries = tile_blocks[0, 0]
    tile_count, list_len = entries.shape
    stripe_no = tile_list // per_row
    column_no = tile_list % per_row
    shifted_no = (stripe_no - quarter) % cells
    anchor_x = 16 * column_no
    anchor_y = 16 * (shifted_no % half)
    view_side = shifted_no // half
    pixels = jnp.arange(256, dtype=jnp.int32)
    across_x = (anchor_x[:, None] + pixels[None, :] % 16).astype(jnp.float32)
    across_y = (anchor_y[:, None] + pixels[None, :] // 16).astype(jnp.float32)
    is_live = (entries >= 0).reshape(-1)
    keep_live = (entries >= 0).astype(jnp.float32)
    block_ids = jnp.maximum(entries, 0).reshape(-1)
    owner_flat = block_ids // blocks
    local_slot = block_ids % blocks
    serial = jnp.arange(tile_count * list_len, dtype=jnp.int32)
    earlier = (
        (owner_flat[:, None] == owner_flat[None, :])
        & is_live[None, :]
        & (serial[None, :] < serial[:, None])
    )
    rank_of = jnp.sum(earlier.astype(jnp.int32), axis=1)
    mailbox = owner_flat * capacity + rank_of
    send_box = jnp.where(is_live, mailbox, devices * capacity)
    read_box = jnp.where(is_live, mailbox, 0)
    request_codes = local_slot + blocks * jnp.repeat(view_side, list_len)
    asks = (
        jnp.full((devices * capacity,), -1, jnp.int32)
        .at[send_box]
        .set(request_codes, mode="drop")
        .reshape(cells, groups, capacity)
    )
    source_group = lax.broadcasted_iota(jnp.int32, (cells, groups, capacity), 1).reshape(-1)
    upper = (jnp.arange(GBLK)[:, None] < jnp.arange(GBLK)[None, :]).astype(jnp.float32)
    log_trans = jnp.zeros((tile_count, 256), jnp.float32)
    colour = jnp.zeros((tile_count, 3, 256), jnp.float32)
    incoming = lax.all_to_all(
        lax.all_to_all(asks, "cell", split_axis=0, concat_axis=0, tiled=True),
        "view",
        split_axis=1,
        concat_axis=1,
        tiled=True,
    )
    served = request_lookup(incoming.reshape(-1), source_group, gauss_params, visible, cameras)
    served = served.reshape(cells, groups, capacity, 9, GBLK)
    returned = lax.all_to_all(
        lax.all_to_all(served, "cell", split_axis=0, concat_axis=0, tiled=True),
        "view",
        split_axis=1,
        concat_axis=1,
        tiled=True,
    )
    lookup = returned.reshape(devices * capacity, 9, GBLK)[read_box].reshape(
        tile_count, list_len, 9, GBLK
    )
    for number in range(list_len):
        features = lookup[:, number]
        features = features.at[:, 5].multiply(keep_live[:, number][:, None])
        log_trans, colour = blend_slot(features, across_x, across_y, log_trans, colour, upper)
    spread = -(-tile_count // cells)
    serial_tiles = jnp.arange(tile_count, dtype=jnp.int32)
    same_stripe = (stripe_no[:, None] == stripe_no[None, :]) & (
        serial_tiles[None, :] < serial_tiles[:, None]
    )
    tile_rank = jnp.sum(same_stripe.astype(jnp.int32), axis=1)
    tile_box = stripe_no * spread + tile_rank
    out_pixels = (
        jnp.zeros((cells * spread, 3, 256), jnp.float32)
        .at[tile_box]
        .set(colour)
        .reshape(cells, spread, 3, 256)
    )
    out_columns = (
        jnp.full((cells * spread,), -1, jnp.int32)
        .at[tile_box]
        .set(column_no)
        .reshape(cells, spread)
    )
    got_pixels, got_columns = (
        lax.all_to_all(out_pixels, "cell", split_axis=0, concat_axis=0, tiled=True),
        lax.all_to_all(out_columns, "cell", split_axis=0, concat_axis=0, tiled=True),
    )
    flat_columns = got_columns.reshape(-1)
    place = jnp.where(flat_columns >= 0, flat_columns, per_row)
    stripe_tiles = (
        jnp.zeros((per_row, 3, 256), jnp.float32)
        .at[place]
        .set(got_pixels.reshape(-1, 3, 256), mode="drop")
    )
    stripe_image = (
        stripe_tiles.reshape(per_row, 3, 16, 16).transpose(1, 2, 0, 3).reshape(3, 16, per_row * 16)
    )
    both = jnp.stack([stripe_image, target[0]])
    padded = with_halo(both, (("cell", 2),), 5)
    row_pos = (my_cell - quarter) % cells % half
    row_index = jnp.arange(padded.shape[2], dtype=jnp.int32)
    keep_rows = ((row_index >= 5) | (row_pos != 0)) & ((row_index < 21) | (row_pos != half - 1))
    padded = padded * keep_rows.astype(jnp.float32)[None, None, :, None]
    loss_rows = stripe_loss(padded[0], padded[1], 16)
    return (stripe_image[None], loss_rows[None])


def solution(mesh):
    return jax.shard_map(
        local,
        mesh=mesh,
        in_specs=(
            P(None, ("cell", "view")),
            P(None, ("cell", "view")),
            P(),
            P("cell", "view", None),
            P("cell", "view", None, None),
            P("view", None, "cell", None),
        ),
        out_specs=(P("view", None, "cell", None), P("view", "cell", None)),
        check_vma=False,
    )
```

profile of v0, /device:TPU:1, one launch (start us, length us, event | category | flops | bytes accessed | tf_op | source)
XLA Modules:
  0.0 386.6 jit_solution(9532526858171762676)
XLA Ops:
  0.6 1.3 compare_and_fusion.1
  2.0 0.7 maximum_remainder_fusion.1
  3.5 1.3 broadcast_multiply_fusion.8
  6.6 1.3 scatter_custom_fusion.1
  8.0 0.8 reshape.1499
  8.7 16.3 %all-to-all-start.1 = ((s32[128,2,1]{1,2,0:T(1,128)}), s32[128,2,1]{1,2,0:T(1,128)S(1)}, u32[]{:S(2)}, u32[]{:S(2)}) async-start(s32[128,2,1]{1,2,0:T(1,128)} %bitcast.11), calls=%async_computation.1 | async-start | bytes 131072 | tf_op jit(solution)/shard_map/all_to_all | solution.py:303
  25.4 0.8 copy.154
  26.2 5.3 %reshape.1500 = f32[59,150,128]{2,1,0:T(8,128)} reshape(f32[59,19200]{1,0:T(8,128)} %param.10) | data formatting | bytes 9062400 | tf_op jit(solution)/shard_map/reshape | solution.py:206
  31.4 5.5 %copy.156 = f32[59,150,128]{2,0,1:T(8,128)} copy(f32[59,150,128]{2,1,0:T(8,128)} %reshape.1500) | data formatting | bytes 9062400 | tf_op jit(solution)/shard_map/reshape | solution.py:206
  37.0 4.8 %all_to_all.37 = s32[128,2,1]{0,2,1:T(1,128)S(1)} all-to-all(s32[128,2,1]{0,2,1:T(1,128)S(1)} %copy.150), channel_id=1, replica_groups=mesh['cell'=128,'view'=2] {'view'}, dimensions={1} | all-to-all | bytes 2048 | tf_op jit(solution)/shard_map/all_to_all | solution.py:302
  45.0 6.8 %gather_fusion = f32[256,59,128]{2,1,0:T(8,128)} fusion(f32[59,150,128]{2,0,1:T(8,128)} %copy.156, s32[1024]{0:T(1024)S(1)} %pad_clamp_fusion.1), kind=kCustom, calls=%fused_computation | custom fusion | bytes 15467520 | tf_op jit(solution)/shard_map/gather | solution.py:206
  51.8 9.8 %fusion.102 = (f32[256,1,128]{2,1,0:T(1,128)}, f32[256,1,128]{2,1,0:T(1,128)S(1)}, f32[256,1,128]{2,1,0:T(1,128)S(1)}, f32[256,1,128]{2,1,0:T(1,128)S(1)}, f32[2...) fusion(f32[256,59,128]{2,1,0:T(8,128)} %gather_fusion), kind=kLoop, calls=%fused_computation.292 | loop fusion | bytes 4980736 | tf_op jit(solution)/shard_map/slice | solution.py:150
  61.6 1.9 fusion.103
  63.4 9.3 %fusion.101 = (f32[256,1,128]{2,1,0:T(1,128)S(1)}, f32[256,1,128]{2,1,0:T(1,128)S(1)}, f32[256,1,128]{2,1,0:T(1,128)S(1)}, f32[256,1,128]{2,1,0:T(1,128)S(1)}, f...) fusion(f32[256,59,128]{2,1,0:T(8,128)} %gather_fusion), kind=kLoop, calls=%fused_computation.291 | loop fusion | bytes 4980736 | tf_op jit(solution)/shard_map/slice | solution.py:150
  72.7 9.5 %fusion.100 = (f32[256,1,128]{2,1,0:T(1,128)}, f32[256,1,128]{2,1,0:T(1,128)}, f32[256,1,128]{2,1,0:T(1,128)}, f32[256,1,128]{2,1,0:T(1,128)}, f32[256,1,128]{2,...) fusion(f32[256,59,128]{2,1,0:T(8,128)} %gather_fusion), kind=kLoop, calls=%fused_computation.290 | loop fusion | bytes 4980736 | tf_op jit(solution)/shard_map/slice | solution.py:150
  83.3 1.2 multiply_add_fusion.5
  84.5 1.2 multiply_add_fusion.4
  86.3 0.8 copy.170
  87.1 0.7 reshape.1511
  87.8 1.2 multiply_add_fusion.9
  89.0 1.2 multiply_add_fusion.11
  90.9 1.4 fusion.71
  93.0 0.7 constant_dynamic-update-slice_fusion.5
  94.4 2.0 gather_fusion.1
  96.4 1.1 fusion.66
  97.5 0.7 constant_dynamic-update-slice_fusion.3
  98.2 2.1 add_maximum_fusion
  100.4 1.6 add_maximum_fusion.2
  103.1 0.7 constant_dynamic-update-slice_fusion.1
  103.8 0.7 constant_dynamic-update-slice_fusion
  104.4 13.6 %all-to-all-start.3 = ((f32[128,2,1,9,128]{4,1,3,2,0:T(2,128)}), f32[128,2,1,9,128]{4,1,3,2,0:T(2,128)S(1)}, u32[]{:S(2)}, u32[]{:S(2)}) async-start(f32[128,2,1,9,128]{4,1,3,2,0:T(2,128)} %constant_dynamic-update-slice_fusion), calls=%async_computation.3 | async-start | bytes 2359296 | tf_op jit(solution)/shard_map/all_to_all | solution.py:312
  118.3 1.1 scatter_custom_fusion
  119.4 0.7 copy.141
  120.3 29.6 %all-to-all-done.3 = f32[128,2,1,9,128]{4,1,3,2,0:T(2,128)S(1)} async-done(((f32[128,2,1,9,128]{4,1,3,2,0:T(2,128)}), f32[128,2,1,9,128]{4,1,3,2,0:T(2,128)S(1)}, u32[]{:S(2)}, u32[]{:S(2)}) %all-to-all-start.3) | async-done | bytes 1179680 | tf_op jit(solution)/shard_map/all_to_all | solution.py:312
  150.1 8.2 %all_to_all.38 = f32[128,2,1,9,128]{4,0,3,2,1:T(8,128)} all-to-all(f32[128,2,1,9,128]{4,0,3,2,1:T(8,128)S(1)} %copy.229), channel_id=1, replica_groups=mesh['cell'=128,'view'=2] {'view'}, dimensions={1} | all-to-all | bytes 2359296 | tf_op jit(solution)/shard_map/all_to_all | solution.py:311
  158.3 6.1 %all-to-all-start = ((s32[128,1,1]{2,1,0:T(1,128)}), s32[128,1,1]{2,1,0:T(1,128)S(1)}, u32[]{:S(2)}, u32[]{:S(2)}) async-start(s32[128,1,1]{2,1,0:T(1,128)} %copy.141), calls=%async_computation | async-start | bytes 131072 | tf_op jit(solution)/shard_map/all_to_all | solution.py:346
  164.5 2.0 copy.230
  166.5 2.3 gather_fusion.2
  168.8 1.9 copy.231
  170.7 0.9 fusion.105
  172.1 17.0 %fusion.20 = f32[120,256]{1,0:T(8,128)S(1)} fusion(f32[120,128]{1,0:T(8,128)S(1)} %bitcast.375, f32[120,128]{1,0:T(8,128)S(1)} %bitcast.378, f32[120,256]{1,0:T(8,128)S(1)} %get-tuple-element.190, f32[120,128]{1,0:T(8,128)S(1)} %bitcast.381, f32[120,128]{1,0:T(8,128)S(1)} %bitcast.384, f32[120,256]{1,0:T(8,128)S(1)} %get-tuple-element.191, ...), kind=kLoop, calls=%fused_computation.40 | loop fusion | flops 55019520 | bytes 737280 | tf_op jit(solution)/shard_map/reduce_sum | solution.py:196
  189.2 20.0 %fusion.21 = f32[120,256,128]{2,1,0:T(8,128)S(1)} fusion(f32[120,128]{1,0:T(8,128)S(1)} %bitcast.376, f32[120,128]{1,0:T(8,128)S(1)} %bitcast.379, f32[120,256]{1,0:T(8,128)S(1)} %get-tuple-element.190, f32[120,128]{1,0:T(8,128)S(1)} %bitcast.382, f32[120,128]{1,0:T(8,128)S(1)} %bitcast.385, f32[120,256]{1,0:T(8,128)S(1)} %get-tuple-element.191, ...), kind=kOutput, calls=%fused_computation.41 | convolution fusion | flops 6090932224 | bytes 16343040 | tf_op jit(solution)/shard_map/tpg,gh->tph/dot_general | solution.py:187
  209.6 20.2 %fusion.14 = f32[120,256,128]{2,1,0:T(8,128)S(1)} fusion(f32[120,128]{1,0:T(8,128)S(1)} %bitcast.389, f32[120,128]{1,0:T(8,128)S(1)} %bitcast.391, f32[120,128]{1,0:T(8,128)S(1)} %bitcast.393, f32[120,128]{1,0:T(8,128)S(1)} %bitcast.395, f32[120,128]{1,0:T(8,128)S(1)} %bitcast.387, f32[120,128]{1,0:T(8,128)S(1)} %broadcast_multiply_fusion, ...), kind=kOutput, calls=%fused_computation.33 | convolution fusion | flops 6090932224 | bytes 16343040 | tf_op jit(solution)/shard_map/tpg,gh->tph/dot_general | solution.py:187
  229.8 29.9 %fusion.10 = f32[120,3,256]{2,1,0:T(4,128)S(1)} fusion(f32[120,256,128]{2,1,0:T(8,128)S(1)} %fusion.14, f32[120,256]{1,0:T(8,128)S(1)} %fusion.20, f32[120,128]{1,0:T(8,128)S(1)} %bitcast.390, f32[120,128]{1,0:T(8,128)S(1)} %bitcast.392, f32[120,128]{1,0:T(8,128)S(1)} %bitcast.394, f32[120,128]{1,0:T(8,128)S(1)} %bitcast.396, f32[120,128]{1,0:T(8,128)S(1)} %bitcast.388, ...), kind=kOutput, calls=%fused_computation.29 | convolution fusion | flops 196608000 | bytes 17080320 | tf_op jit(solution)/shard_map/tpg,tcg->tcp/dot_general | solution.py:193
  259.8 25.4 %fusion.44 = f32[120,3,256]{2,1,0:T(4,128)S(1)} fusion(f32[120,3,256]{2,1,0:T(4,128)S(1)} %fusion.10, f32[120,256,128]{2,1,0:T(8,128)S(1)} %fusion.21, f32[120,128]{1,0:T(8,128)S(1)} %bitcast.377, f32[120,128]{1,0:T(8,128)S(1)} %bitcast.380, f32[120,256]{1,0:T(8,128)S(1)} %get-tuple-element.190, f32[120,128]{1,0:T(8,128)S(1)} %bitcast.383, ...), kind=kOutput, calls=%fused_computation.78 | convolution fusion | flops 192768000 | bytes 17448960 | tf_op jit(solution)/shard_map/tpg,tcg->tcp/dot_general | solution.py:193
  285.2 4.4 %scatter_fusion = f32[128,3,256]{2,1,0:T(4,128)S(1)} fusion(f32[128,3,256]{2,1,0:T(4,128)S(1)} %broadcast_in_dim.21, s32[120]{0:T(128)S(1)} %fusion.86, f32[120,3,256]{2,1,0:T(4,128)S(1)} %fusion.44), kind=kCustom, calls=%fused_computation.5 | custom fusion | bytes 1106400 | tf_op jit(solution)/shard_map/scatter | solution.py:335
  289.6 1.2 copy.234
  290.8 13.4 %all-to-all-start.5 = ((f32[128,1,3,256]{3,1,2,0:T(1,128)}), f32[128,1,3,256]{3,1,2,0:T(1,128)S(1)}, u32[]{:S(2)}, u32[]{:S(2)}) async-start(f32[128,1,3,256]{3,1,2,0:T(1,128)} %copy.234), calls=%async_computation.5 | async-start | bytes 786432 | tf_op jit(solution)/shard_map/all_to_all | solution.py:345
  304.8 2.3 reduce.4
  307.2 12.9 %all-to-all-done.5 = f32[128,1,3,256]{3,1,2,0:T(1,128)S(1)} async-done(((f32[128,1,3,256]{3,1,2,0:T(1,128)}), f32[128,1,3,256]{3,1,2,0:T(1,128)S(1)}, u32[]{:S(2)}, u32[]{:S(2)}) %all-to-all-start.5) | async-done | bytes 393248 | tf_op jit(solution)/shard_map/all_to_all | solution.py:345
  320.5 4.3 %scatter_fusion.1 = f32[120,3,256]{2,1,0:T(4,128)S(1)} fusion(f32[120,3,256]{2,1,0:T(4,128)S(1)} %broadcast_in_dim.18, s32[128]{0:T(128)S(1)} %fusion.87, f32[128,3,256]{2,1,0:T(4,128)S(1)} %copy.236), kind=kCustom, calls=%fused_computation.6 | custom fusion | bytes 1180160 | tf_op jit(solution)/shard_map/scatter | solution.py:353
  324.8 1.0 copy.237
  325.8 1.9 copy.238
  327.7 1.5 broadcast_in_dim_reshape.4
  329.2 1.0 constant_dynamic-update-slice_fusion.10
  330.2 1.0 constant_dynamic-update-slice_fusion.9
  331.3 1.3 collective-permute-start.1
  334.2 4.3 %collective-permute-done.1 = f32[2,3,5,1920]{3,2,1,0:T(8,128)S(1)} collective-permute-done((f32[2,3,5,1920]{3,2,1,0:T(8,128)S(1)}, f32[2,3,5,1920]{3,2,1,0:T(8,128)S(1)}, u32[]{:S(2)}, u32[]{:S(2)}) %collective-permute-start.1) | collective-permute-done | bytes 230432 | tf_op jit(solution)/shard_map/ppermute | solution.py:18
  338.5 6.7 %collective-permute-done = f32[2,3,5,1920]{3,2,1,0:T(8,128)S(1)} collective-permute-done((f32[2,3,5,1920]{3,2,1,0:T(8,128)S(1)}, f32[2,3,5,1920]{3,2,1,0:T(8,128)S(1)}, u32[]{:S(2)}, u32[]{:S(2)}) %collective-permute-start) | collective-permute-done | bytes 230432 | tf_op jit(solution)/shard_map/ppermute | solution.py:16
  345.5 1.2 slice_bitcast_fusion.1
  346.9 17.9 %multiply_add_fusion = f32[5,3,26,1920]{3,2,1,0:T(8,128)} fusion(f32[5,3,26,1920]{3,2,1,0:T(8,128)S(1)} %pad_maximum_fusion, f32[]{:T(128)} %bitcast.92, f32[]{:T(128)} %bitcast.91, f32[]{:T(128)} %bitcast.90, f32[]{:T(128)} %bitcast.89, f32[]{:T(128)} %bitcast.88, f32[]{:T(128)} %bitcast.87, f32[]{:T(128)} %bitcast.86, f32[]{:T(128)} %bitcast.85, ...), kind=kLoop, calls=%fused_computation.44 | loop fusion | flops 15724800 | bytes 5990444 | tf_op jit(solution)/shard_map/add | solution.py:230
  364.8 19.2 %fusion.34 = f32[5,3,16,1920]{3,2,1,0:T(8,128)S(1)} fusion(f32[5,3,26,1920]{3,2,1,0:T(8,128)} %multiply_add_fusion, f32[]{:T(128)} %bitcast.92, f32[]{:T(128)} %bitcast.91, f32[]{:T(128)} %bitcast.90, f32[]{:T(128)} %bitcast.89, f32[]{:T(128)} %bitcast.88, f32[]{:T(128)} %bitcast.87, f32[]{:T(128)} %bitcast.86, f32[]{:T(128)} %bitcast.85, f32[]{:T(128)} %bitcast.84, ...), kind=kLoop, calls=%fused_computation.57 | loop fusion | flops 9676800 | bytes 22118444 | tf_op jit(solution)/shard_map/add | solution.py:231
  384.3 1.2 fusion.58
  385.4 0.7 add_bitcast_fusion
  (124 shorter events, 16.0 us)
Async XLA Ops:
  0.6 93.8 %copy-start = (s32[4,19200]{1,0:T(4,128)S(1)}, s32[4,19200]{1,0:T(4,128)}, u32[]{:S(2)}) copy-start(s32[4,19200]{1,0:T(4,128)} %param.11) | copy-start | bytes 921604
  8.7 28.2 %all-to-all-start.1 = ((s32[128,2,1]{1,2,0:T(1,128)}), s32[128,2,1]{1,2,0:T(1,128)S(1)}, u32[]{:S(2)}, u32[]{:S(2)}) async-start(s32[128,2,1]{1,2,0:T(1,128)} %bitcast.11), calls=%async_computation.1 | async-start | bytes 131072 | tf_op jit(solution)/shard_map/all_to_all | solution.py:303
  87.8 8.6 %copy-start.11 = (f32[256]{0:T(256)S(1)}, f32[256]{0:T(256)}, u32[]{:S(2)}) copy-start(f32[256]{0:T(256)} %reshape.1511) | copy-start | bytes 3076
  87.8 10.4 %copy-start.12 = (f32[256,1]{0,1:T(1,128)S(1)}, f32[256,1]{0,1:T(1,128)}, u32[]{:S(2)}) copy-start(f32[256,1]{0,1:T(1,128)} %get-tuple-element.144) | copy-start | bytes 3076
  87.8 10.4 %copy-start.13 = (f32[256,1]{0,1:T(1,128)S(1)}, f32[256,1]{0,1:T(1,128)}, u32[]{:S(2)}) copy-start(f32[256,1]{0,1:T(1,128)} %get-tuple-element.146) | copy-start | bytes 3076
  87.8 10.4 %copy-start.14 = (f32[256,1]{0,1:T(1,128)S(1)}, f32[256,1]{0,1:T(1,128)}, u32[]{:S(2)}) copy-start(f32[256,1]{0,1:T(1,128)} %get-tuple-element.147) | copy-start | bytes 3076
  90.2 6.2 %copy-start.10 = (f32[256,1,128]{2,1,0:T(1,128)S(1)}, f32[256,1,128]{2,1,0:T(1,128)}, u32[]{:S(2)}) copy-start(f32[256,1,128]{2,1,0:T(1,128)} %get-tuple-element.104) | copy-start | bytes 393220
  92.3 8.0 %copy-start.2 = (f32[256,1,128]{2,1,0:T(1,128)S(1)}, f32[256,1,128]{2,1,0:T(1,128)}, u32[]{:S(2)}) copy-start(f32[256,1,128]{2,1,0:T(1,128)} %get-tuple-element.99) | copy-start | bytes 393220
  92.3 8.0 %copy-start.3 = (f32[256,1,128]{2,1,0:T(1,128)S(1)}, f32[256,1,128]{2,1,0:T(1,128)}, u32[]{:S(2)}) copy-start(f32[256,1,128]{2,1,0:T(1,128)} %get-tuple-element.100) | copy-start | bytes 393220
  92.3 8.0 %copy-start.4 = (f32[256,1,128]{2,1,0:T(1,128)S(1)}, f32[256,1,128]{2,1,0:T(1,128)}, u32[]{:S(2)}) copy-start(f32[256,1,128]{2,1,0:T(1,128)} %get-tuple-element.101) | copy-start | bytes 393220
  92.3 8.0 %copy-start.5 = (f32[256,1,128]{2,1,0:T(1,128)S(1)}, f32[256,1,128]{2,1,0:T(1,128)}, u32[]{:S(2)}) copy-start(f32[256,1,128]{2,1,0:T(1,128)} %get-tuple-element.102) | copy-start | bytes 393220
  96.4 6.3 %copy-start.6 = (f32[256,1,128]{2,1,0:T(1,128)S(1)}, f32[256,1,128]{2,1,0:T(1,128)}, u32[]{:S(2)}) copy-start(f32[256,1,128]{2,1,0:T(1,128)} %get-tuple-element.56) | copy-start | bytes 393220
  96.4 6.3 %copy-start.7 = (f32[256,1,128]{2,1,0:T(1,128)S(1)}, f32[256,1,128]{2,1,0:T(1,128)}, u32[]{:S(2)}) copy-start(f32[256,1,128]{2,1,0:T(1,128)} %get-tuple-element.72) | copy-start | bytes 393220
  96.4 6.3 %copy-start.8 = (f32[256,1,128]{2,1,0:T(1,128)S(1)}, f32[256,1,128]{2,1,0:T(1,128)}, u32[]{:S(2)}) copy-start(f32[256,1,128]{2,1,0:T(1,128)} %get-tuple-element.73) | copy-start | bytes 393220
  96.4 6.3 %copy-start.9 = (f32[256,1,128]{2,1,0:T(1,128)S(1)}, f32[256,1,128]{2,1,0:T(1,128)}, u32[]{:S(2)}) copy-start(f32[256,1,128]{2,1,0:T(1,128)} %get-tuple-element.74) | copy-start | bytes 393220
  100.4 17.7 %copy-start.20 = (s32[120]{0:T(128)S(1)}, s32[120]{0:T(128)}, u32[]{:S(2)}) copy-start(s32[120]{0:T(128)} %get-tuple-element.189) | copy-start | bytes 1444
  100.4 17.9 %copy-start.19 = (s32[1,1,120]{2,1,0:T(1,128)S(1)}, s32[1,1,120]{2,1,0:T(1,128)}, u32[]{:S(2)}) copy-start(s32[1,1,120]{2,1,0:T(1,128)} %param.13) | copy-start | bytes 1444
  100.4 19.8 %copy-start.16 = (s32[240,1]{0,1:T(1,128)S(1)}, s32[240,1]{0,1:T(1,128)}, u32[]{:S(2)}) copy-start(s32[240,1]{0,1:T(1,128)} %get-tuple-element.163) | copy-start | bytes 2884
  100.4 19.8 %copy-start.15 = (f32[120,2]{0,1:T(2,128)S(1)}, f32[120,2]{0,1:T(2,128)}, u32[]{:S(2)}) copy-start(f32[120,2]{0,1:T(2,128)} %get-tuple-element.174) | copy-start | bytes 2884
  100.4 19.8 %copy-start.17 = (s32[120]{0:T(128)S(1)}, s32[120]{0:T(128)}, u32[]{:S(2)}) copy-start(s32[120]{0:T(128)} %get-tuple-element.26) | copy-start | bytes 1444
  100.4 19.8 %copy-start.18 = (s32[120]{0:T(128)S(1)}, s32[120]{0:T(128)}, u32[]{:S(2)}) copy-start(s32[120]{0:T(128)} %get-tuple-element.187) | copy-start | bytes 1444
  104.4 45.5 %all-to-all-start.3 = ((f32[128,2,1,9,128]{4,1,3,2,0:T(2,128)}), f32[128,2,1,9,128]{4,1,3,2,0:T(2,128)S(1)}, u32[]{:S(2)}, u32[]{:S(2)}) async-start(f32[128,2,1,9,128]{4,1,3,2,0:T(2,128)} %constant_dynamic-update-slice_fusion), calls=%async_computation.3 | async-start | bytes 2359296 | tf_op jit(solution)/shard_map/all_to_all | solution.py:312
  158.3 132.5 %all-to-all-start = ((s32[128,1,1]{2,1,0:T(1,128)}), s32[128,1,1]{2,1,0:T(1,128)S(1)}, u32[]{:S(2)}, u32[]{:S(2)}) async-start(s32[128,1,1]{2,1,0:T(1,128)} %copy.141), calls=%async_computation | async-start | bytes 131072 | tf_op jit(solution)/shard_map/all_to_all | solution.py:346
  290.8 29.4 %all-to-all-start.5 = ((f32[128,1,3,256]{3,1,2,0:T(1,128)}), f32[128,1,3,256]{3,1,2,0:T(1,128)S(1)}, u32[]{:S(2)}, u32[]{:S(2)}) async-start(f32[128,1,3,256]{3,1,2,0:T(1,128)} %copy.234), calls=%async_computation.5 | async-start | bytes 786432 | tf_op jit(solution)/shard_map/all_to_all | solution.py:345
  331.3 7.2 %collective-permute-start.1 = (f32[2,3,5,1920]{3,2,1,0:T(8,128)S(1)}, f32[2,3,5,1920]{3,2,1,0:T(8,128)S(1)}, u32[]{:S(2)}, u32[]{:S(2)}) collective-permute-start(f32[2,3,5,1920]{3,2,1,0:T(8,128)S(1)} %get-tuple-element.139), channel_id=1, source_target_pairs={{2,0},{4,2},{6,4},{8,6},{10,8},{12,10},{14,12},{16,14},{18,16},{20... | collective-permute-start | bytes 691208 | tf_op jit(solution)/shard_map/ppermute | solution.py:18
  332.6 12.6 %collective-permute-start = (f32[2,3,5,1920]{3,2,1,0:T(8,128)S(1)}, f32[2,3,5,1920]{3,2,1,0:T(8,128)S(1)}, u32[]{:S(2)}, u32[]{:S(2)}) collective-permute-start(f32[2,3,5,1920]{3,2,1,0:T(8,128)S(1)} %get-tuple-element.138), channel_id=1, source_target_pairs={{0,2},{2,4},{4,6},{6,8},{8,10},{10,12},{12,14},{14,16},{16,18},{18... | collective-permute-start | bytes 691208 | tf_op jit(solution)/shard_map/ppermute | solution.py:16
  364.8 21.3 %copy-start.1 = (s32[4,19200]{1,0:T(4,128)S(1)}, s32[4,19200]{1,0:T(4,128)}, u32[]{:S(2)}) copy-start(s32[4,19200]{1,0:T(4,128)} %param.11) | copy-start | bytes 921604
where the time goes:
time: 393 us; the launch traced here: 387 us
  matrix products  95.5 us (24%)
  local copies, waits for them, and re-layouts  91.8 us (23%)
  other arithmetic  79.8 us (20%)
  waiting for transfers between devices  53.6 us (14%)
  starting transfers between devices  51.1 us (13%)
  blocking collectives  13.1 us (3%)
    dot_general x2, matrix products, blend_slot(): jnp.einsum('tpg,tcg->tcp', weights, features[:, 6:9], precision=lax.Preci...  55.3 us
    dot_general x2, matrix products, before_sums(): jnp.einsum('tpg,gh->tph', log_keep, upper, precision=lax.Precision.HIGHEST)  40.2 us
    all_to_all x1, waiting for transfers between devices, local(): lax.all_to_all(served, 'cell', split_axis=0, concat_axis=0, tiled=True)  29.6 us
    slice x3, local copies, waits for them, and re-layouts, project(): raw_params[:, 11 + 3 * number + channel]  28.5 us
    add x1, other arithmetic, blur(): sum((taps[number] * across[..., number:number + row_count, :] for number...  19.2 us
    add x1, other arithmetic, blur(): sum((taps[number] * wide[..., number:number + columns] for number in rang...  17.9 us
    reduce_sum x1, other arithmetic, blend_slot(): return (log_trans + jnp.sum(log_keep, axis=2), colour)  17 us
    all_to_all x1, starting transfers between devices, local(): lax.all_to_all(asks, 'cell', split_axis=0, concat_axis=0, tiled=True)  16.3 us
  transfers between devices with their start and end apart: 6, of which 4 were waited for; matrix products, arithmetic and copies ran while one was open for 37% of the time, Pallas kernels for 0%

commit v1 on v0

v1 whole, which is shorter than its diff:
```python
import functools

import jax
import jax.numpy as jnp
from jax import lax
from jax.experimental import pallas as pl
from jax.experimental.pallas import tpu as pltpu
from jax.sharding import PartitionSpec as P

MESH = pl.DeviceIdType.MESH
F32 = jnp.float32
BF16 = jnp.bfloat16
LOG2E = 1.4426950408889634
NEG = -1e30
NB = 150
NBP = 152
CELLS = 128
TILES = 120


def dot00(left, right):
    return lax.dot_general(left, right, (((0,), (0,)), ((), ())), preferred_element_type=F32)


def dot10(left, right):
    return lax.dot_general(left, right, (((1,), (0,)), ((), ())), preferred_element_type=F32)


def pieces(value):
    high = value.astype(BF16)
    rest = value - high.astype(F32)
    mid = rest.astype(BF16)
    low = (rest - mid.astype(F32)).astype(BF16)
    return high, mid, low


def iota(shape, dim):
    return lax.broadcasted_iota(jnp.int32, shape, dim)


def quotient(value, divisor):
    return ((value.astype(F32) + 0.5) * (1.0 / divisor)).astype(jnp.int32)


def harmonics(ux, uy, uz):
    xx, yy, zz = ux * ux, uy * uy, uz * uz
    return [
        None,
        -0.4886025119029199 * uy,
        0.4886025119029199 * uz,
        -0.4886025119029199 * ux,
        1.0925484305920792 * ux * uy,
        -1.0925484305920792 * uy * uz,
        0.31539156525252005 * (2.0 * zz - xx - yy),
        -1.0925484305920792 * ux * uz,
        0.5462742152960396 * (xx - yy),
        -0.5900435899266435 * uy * (3.0 * xx - yy),
        2.890611442640554 * ux * uy * uz,
        -0.4570457994644658 * uy * (4.0 * zz - xx - yy),
        0.3731763325901154 * uz * (2.0 * zz - 3.0 * xx - 3.0 * yy),
        -0.4570457994644658 * ux * (4.0 * zz - xx - yy),
        1.445305721320277 * uz * (xx - yy),
        -0.5900435899266435 * ux * (xx - 3.0 * yy),
    ]


def project_chunk(raw, seen, cam, view):
    def pick(entry):
        return jnp.where(
            view < 1.5,
            jnp.where(view < 0.5, cam[0, entry], cam[1, entry]),
            jnp.where(view < 2.5, cam[2, entry], cam[3, entry]),
        )

    e = [pick(entry) for entry in range(15)]
    rot = [e[0:3], e[3:6], e[6:9]]
    off = e[9:12]
    focal = e[12]
    pos = [raw(n) for n in range(3)]
    pc = [rot[m][0] * pos[0] + rot[m][1] * pos[1] + rot[m][2] * pos[2] + off[m] for m in range(3)]
    inv_z = 1.0 / pc[2]
    fz = focal * inv_z
    sx = focal * pc[0] / pc[2] + e[13]
    sy = focal * pc[1] / pc[2] + e[14]
    q = [raw(6 + n) for n in range(4)]
    scale = 1.0 / jnp.sqrt(q[0] * q[0] + q[1] * q[1] + q[2] * q[2] + q[3] * q[3])
    r, x, y, z = [part * scale for part in q]
    turn = [
        [1.0 - 2.0 * (y * y + z * z), 2.0 * (x * y - r * z), 2.0 * (x * z + r * y)],
        [2.0 * (x * y + r * z), 1.0 - 2.0 * (x * x + z * z), 2.0 * (y * z - r * x)],
        [2.0 * (x * z - r * y), 2.0 * (y * z + r * x), 1.0 - 2.0 * (x * x + y * y)],
    ]
    sq = [jnp.exp(2.0 * raw(3 + n)) for n in range(3)]
    jz = [-fz * pc[0] * inv_z, -fz * pc[1] * inv_z]
    cams = [[fz * rot[m][k] + jz[m] * rot[2][k] for k in range(3)] for m in range(2)]
    w = [
        [cams[m][0] * turn[0][k] + cams[m][1] * turn[1][k] + cams[m][2] * turn[2][k] for k in range(3)]
        for m in range(2)
    ]
    s0 = [sq[k] * w[0][k] for k in range(3)]
    cov_a = s0[0] * w[0][0] + s0[1] * w[0][1] + s0[2] * w[0][2] + 0.3
    cov_b = s0[0] * w[1][0] + s0[1] * w[1][1] + s0[2] * w[1][2]
    cov_c = sq[0] * w[1][0] * w[1][0] + sq[1] * w[1][1] * w[1][1] + sq[2] * w[1][2] * w[1][2] + 0.3
    inv_det = 1.0 / (cov_a * cov_c - cov_b * cov_b)
    eye = [-(rot[0][k] * off[0] + rot[1][k] * off[1] + rot[2][k] * off[2]) for k in range(3)]
    head = [pos[k] - eye[k] for k in range(3)]
    inv_len = 1.0 / jnp.sqrt(head[0] * head[0] + head[1] * head[1] + head[2] * head[2])
    basis = harmonics(head[0] * inv_len, head[1] * inv_len, head[2] * inv_len)
    colours = []
    for k in range(3):
        total = 0.5 + 0.28209479177387814 * raw(11 + k)
        for j in range(1, 16):
            total = total + basis[j] * raw(11 + 3 * j + k)
        colours.append(jnp.maximum(total, 0.0))
    log_o = jnp.maximum(-LOG2E * jnp.log1p(jnp.exp(-raw(10))), NEG)
    log_o = jnp.where(seen > 0, log_o, NEG)
    return [
        sx,
        sy,
        (-0.5 * LOG2E) * (cov_c * inv_det),
        LOG2E * (cov_b * inv_det),
        (-0.5 * LOG2E) * (cov_a * inv_det),
        log_o,
    ] + colours


def kernel(
    params,
    visible,
    cam,
    tile_ids,
    tile_blocks,
    target,
    image_out,
    loss_out,
    par_s,
    vis_s,
    tid_s,
    req,
    rreq,
    pick1,
    pick2,
    view_s,
    feat,
    grid_f,
    px_s,
    sbuf,
    rbuf,
    s2buf,
    r2buf,
    tpad,
    ipad,
    vert,
    blur_t,
    blur_i,
    load_sem,
    req_send,
    req_recv,
    halo_send,
    halo_recv,
    one_send,
    one_recv,
    two_send,
    two_recv,
    own_sem,
):
    my_c = lax.axis_index("cell")
    my_v = lax.axis_index("view")
    me_slot = my_v * CELLS + my_c

    barrier = pltpu.get_barrier_semaphore()

    def greet(k, carry):
        cell = lax.rem(my_c + k, CELLS)
        pl.semaphore_signal(barrier, inc=1, device_id=(cell, my_v), device_id_type=MESH)
        pl.semaphore_signal(barrier, inc=1, device_id=(cell, 1 - my_v), device_id_type=MESH)
        return carry

    pl.semaphore_signal(barrier, inc=1, device_id=(my_c, 1 - my_v), device_id_type=MESH)
    lax.fori_loop(1, CELLS, greet, 0)

    par_s[:, NB:NBP, :] = jnp.zeros((59, NBP - NB, 128), F32)
    vis_s[:, NB:NBP, :] = jnp.zeros((4, NBP - NB, 128), jnp.int32)

    def load(b, carry):
        lanes = pl.ds(pl.multiple_of(b * 128, 128), 128)
        pltpu.make_async_copy(params.at[:, lanes], par_s.at[:, b, :], load_sem.at[0]).start()
        pltpu.make_async_copy(visible.at[:, lanes], vis_s.at[:, b, :], load_sem.at[1]).start()
        return carry

    lax.fori_loop(0, NB, load, 0)

    tid_s[...] = jnp.full((8, 128), -1.0, F32)
    tid_s[0:1, 0:TILES] = tile_ids[...].astype(F32)
    tid = jnp.transpose(jnp.broadcast_to(tid_s[0:1, :], (128, 128)))[0:TILES, 0:1].astype(jnp.int32)
    stripe = quotient(tid, TILES)
    column = tid - TILES * stripe
    lane2 = iota((TILES, 256), 1)
    hits = []
    local = []
    for entry in range(2):
        block = tile_blocks[:, entry : entry + 1]
        owner = quotient(jnp.maximum(block, 0), NB)
        cell = owner // 2
        slot = (owner - 2 * cell) * CELLS + cell
        hits.append((jnp.where(block >= 0, slot, -1) == lane2).astype(F32))
        local.append((block - NB * owner + 1).astype(F32))
    by_stripe = (stripe == iota((TILES, 128), 1)).astype(F32)
    lb_row = jnp.sum(hits[0] * local[0] + hits[1] * local[1], axis=0, keepdims=True) - 1.0
    tl_row = jnp.sum((hits[0] + hits[1]) * tid.astype(F32), axis=0, keepdims=True)
    col_row = jnp.sum(by_stripe * (column + 1).astype(F32), axis=0, keepdims=True) - 1.0
    sub = iota((128, 128), 0)
    for part in range(2):
        lanes = slice(128 * part, 128 * (part + 1))
        text = jnp.where(
            sub < 32, lb_row[:, lanes], jnp.where(sub < 64, tl_row[:, lanes], col_row)
        )
        req[lanes, 0, :] = jnp.transpose(text).astype(jnp.int32)
    stripe_hot = by_stripe.astype(BF16)
    pick1[...] = dot00(stripe_hot, hits[0].astype(BF16)).astype(BF16)
    pick2[...] = dot00(stripe_hot, hits[1].astype(BF16)).astype(BF16)
    tpad[:, 8:24, :] = target[...]

    pl.semaphore_wait(barrier, 2 * CELLS - 1)

    def exchange(src, dst, rows, send, recv, view, first):
        def go(k, carry):
            cell = lax.rem(my_c + k, CELLS)
            pltpu.make_async_remote_copy(
                src_ref=src.at[view * CELLS + cell, pl.ds(0, rows)],
                dst_ref=dst.at[me_slot, pl.ds(0, rows)],
                send_sem=send,
                recv_sem=recv,
                device_id=(cell, view),
                device_id_type=MESH,
            ).start()
            return carry

        lax.fori_loop(first, CELLS, go, 0)

    def settle(ref, count, rows, sem):
        part = ref.at[pl.ds(0, count), pl.ds(0, rows)]
        pltpu.make_async_copy(part, part, sem).wait()

    def own(src, dst):
        copy = pltpu.make_async_copy(src, dst, own_sem)
        copy.start()
        copy.wait()

    exchange(req, rreq, 1, req_send, req_recv, my_v, 1)
    exchange(req, rreq, 1, req_send, req_recv, 1 - my_v, 0)

    above = lax.rem(my_c + CELLS - 1, CELLS)
    below = lax.rem(my_c + 1, CELLS)

    def halo(buf, number):
        up = pltpu.make_async_remote_copy(
            src_ref=buf.at[:, pl.ds(8, 8), :],
            dst_ref=buf.at[:, pl.ds(24, 8), :],
            send_sem=halo_send.at[2 * number],
            recv_sem=halo_recv.at[2 * number],
            device_id=(above, my_v),
            device_id_type=MESH,
        )
        down = pltpu.make_async_remote_copy(
            src_ref=buf.at[:, pl.ds(16, 8), :],
            dst_ref=buf.at[:, pl.ds(0, 8), :],
            send_sem=halo_send.at[2 * number + 1],
            recv_sem=halo_recv.at[2 * number + 1],
            device_id=(below, my_v),
            device_id_type=MESH,
        )
        up.start()
        down.start()
        return up, down

    target_halo = halo(tpad, 0)
    own(req.at[me_slot], rreq.at[me_slot])
    settle(rreq, 255, 1, req_recv)

    asked = rreq[:, 0, :].astype(F32)
    turned = jnp.concatenate(
        [jnp.transpose(asked[0:128]), jnp.transpose(asked[128:256])], axis=1
    )
    want = turned[0:1, :].astype(jnp.int32)
    tile = turned[32:33, :].astype(jnp.int32)
    cols_in = jnp.where(my_v == 0, turned[64:65, 0:128], turned[64:65, 128:256]).astype(jnp.int32)
    t_stripe = quotient(tile, TILES)
    t_col = tile - TILES * t_stripe
    place = t_stripe - CELLS // 4
    place = jnp.where(place < 0, place + CELLS, place)
    side = (place >= CELLS // 2).astype(jnp.int32)
    anchor_x = (16 * t_col).astype(F32)
    anchor_y = (16 * (place - (CELLS // 2) * side)).astype(F32)
    view_d = (2 * (iota((1, 256), 1) // CELLS) + side).astype(F32)
    hot = (iota((NBP, 256), 0) == want).astype(F32)
    view_s[...] = jnp.broadcast_to(jnp.sum(hot * view_d, axis=1, keepdims=True), (NBP, 128))
    hot16 = hot.astype(BF16)

    pltpu.make_async_copy(par_s.at[:, pl.ds(0, NB), :], par_s.at[:, pl.ds(0, NB), :], load_sem.at[0]).wait()
    pltpu.make_async_copy(vis_s.at[:, pl.ds(0, NB), :], vis_s.at[:, pl.ds(0, NB), :], load_sem.at[1]).wait()

    def project(i, carry):
        rows = pl.ds(pl.multiple_of(8 * i, 8), 8)
        view = view_s[rows, :]
        seen = jnp.where(
            view < 1.5,
            jnp.where(view < 0.5, vis_s[0, rows, :], vis_s[1, rows, :]),
            jnp.where(view < 2.5, vis_s[2, rows, :], vis_s[3, rows, :]),
        )
        found = project_chunk(lambda f: par_s[f, rows, :], seen, cam, view)
        inside = iota((8, 128), 0) + 8 * i < NB
        for f in range(9):
            feat[f, rows, :] = jnp.where(inside, found[f], 0.0)
        return carry

    lax.fori_loop(0, NBP // 8, project, 0)

    live = want >= 0
    for f in range(9):
        high, mid, low = pieces(feat[f])
        got = (dot00(low, hot16) + dot00(mid, hot16)) + dot00(high, hot16)
        if f == 0:
            got = got - anchor_x
        if f == 1:
            got = got - anchor_y
        if f == 5:
            got = jnp.where(live, got, NEG)
        grid_f[0, f] = got[:, 0:128]
        grid_f[1, f] = got[:, 128:256]

    sub8 = iota((8, 128), 0).astype(F32)

    def render(view):
        for quarter in range(4):

            def blend(g, state):
                state = list(state)
                row = [
                    jnp.broadcast_to(grid_f[view, f, pl.ds(g, 1), :], (8, 128)) for f in range(9)
                ]
                dx = [sub8 - row[0], (sub8 + 8.0) - row[0]]
                lead = [row[2] * d * d + row[5] for d in dx]
                cross = [row[3] * d for d in dx]
                for line in range(4):
                    dy = (4.0 * quarter + line) - row[1]
                    bend = row[4] * dy
                    for half in range(2):
                        at = 4 * (2 * line + half)
                        alpha = jnp.exp2(lead[half] + dy * (cross[half] + bend))
                        weight = alpha * state[at + 3]
                        state[at] = state[at] + weight * row[6]
                        state[at + 1] = state[at + 1] + weight * row[7]
                        state[at + 2] = state[at + 2] + weight * row[8]
                        state[at + 3] = state[at + 3] - weight
                return tuple(state)

            zero = jnp.zeros((8, 128), F32)
            one = jnp.ones((8, 128), F32)
            state = lax.fori_loop(0, 128, blend, (zero, zero, zero, one) * 8)
            for at in range(8):
                start = 64 * (quarter % 2) + 8 * at
                for k in range(4):
                    px_s[2 * k + quarter // 2, start : start + 8, :] = state[4 * at + k]
        rows = pl.ds(pl.multiple_of(view * CELLS, CELLS), CELLS)
        for k in range(8):
            sbuf[rows, k, :] = jnp.transpose(px_s[k])

    render(my_v)
    exchange(sbuf, rbuf, 8, one_send, one_recv, my_v, 1)
    own(sbuf.at[me_slot], rbuf.at[me_slot])
    render(1 - my_v)
    exchange(sbuf, rbuf, 8, one_send, one_recv, 1 - my_v, 0)

    taps = [0.0] * 6
    total = sum(2.718281828459045 ** (-(k * k) / 4.5) for k in range(-5, 6))
    for k in range(6):
        taps[k] = 2.718281828459045 ** (-(k * k) / 4.5) / total

    spot = lax.rem(my_c + CELLS - CELLS // 4, CELLS // 2)
    keep_top = jnp.where(spot != 0, 1.0, 0.0)
    keep_bottom = jnp.where(spot != CELLS // 2 - 1, 1.0, 0.0)

    def down_columns(terms):
        totals = [taps[0] * v for v in terms(0)]
        for k in range(1, 6):
            lower, upper = terms(-k), terms(k)
            totals = [t + taps[k] * (a + b) for t, a, b in zip(totals, lower, upper)]
        return totals

    def along_rows(count, out):
        def go(i, carry):
            plane = i // 2
            rows = pl.ds(pl.multiple_of(8 * (i % 2), 8), 8)
            x = vert[plane, rows, :]
            acc = taps[0] * x
            for k in range(1, 6):
                acc = acc + taps[k] * (pltpu.roll(x, k, 1) + pltpu.roll(x, 2048 - k, 1))
            out[plane, rows, :] = acc[:, 0:1920]
            return carry

        lax.fori_loop(0, 2 * count, go, 0)

    for copy in target_halo:
        copy.wait()
    tpad[:, 0:8, :] = tpad[:, 0:8, :] * keep_top
    tpad[:, 24:32, :] = tpad[:, 24:32, :] * keep_bottom
    for plane in range(9):
        vert[plane, :, 1920:2048] = jnp.zeros((16, 128), F32)

    def target_columns(j, carry):
        lanes = pl.ds(pl.multiple_of(128 * j, 128), 128)
        for ch in range(3):

            def terms(k):
                t = tpad[ch, 8 + k : 24 + k, lanes]
                return [t, t * t]

            found = down_columns(terms)
            vert[ch, :, lanes] = found[0]
            vert[3 + ch, :, lanes] = found[1]
        return carry

    lax.fori_loop(0, 15, target_columns, 0)
    along_rows(6, blur_t)

    settle(req, 255, 1, req_send)
    settle(rbuf, 255, 8, one_recv)
    hot1 = pick1[...]
    hot2 = pick2[...]

    def both(k):
        parts = pieces(rbuf[:, k, :])
        first = (dot10(hot1, parts[2]) + dot10(hot1, parts[1])) + dot10(hot1, parts[0])
        if k >= 6:
            return first, None
        second = (dot10(hot2, parts[2]) + dot10(hot2, parts[1])) + dot10(hot2, parts[0])
        return first, second

    clear = [both(6)[0], both(7)[0]]
    for k in range(6):
        first, second = both(k)
        s2buf[:, k, :] = first + clear[k % 2] * second

    def exchange2(k, carry):
        cell = lax.rem(my_c + k, CELLS)
        pltpu.make_async_remote_copy(
            src_ref=s2buf.at[cell, pl.ds(0, 6)],
            dst_ref=r2buf.at[my_c, pl.ds(0, 6)],
            send_sem=two_send,
            recv_sem=two_recv,
            device_id=(cell, my_v),
            device_id_type=MESH,
        ).start()
        return carry

    lax.fori_loop(1, CELLS, exchange2, 0)
    own(s2buf.at[my_c], r2buf.at[my_c])
    settle(sbuf, 255, 8, one_send)
    settle(r2buf, 127, 6, two_recv)

    hot_col = (iota((TILES, 128), 0) == cols_in).astype(BF16)
    sub_b = iota((15, 8, 128), 1)
    lane_b = iota((15, 8, 128), 2) // 16
    for k in range(6):
        parts = pieces(r2buf[:, k, :])
        found = (dot10(hot_col, parts[2]) + dot10(hot_col, parts[1])) + dot10(hot_col, parts[0])
        cube = found.reshape(15, 8, 128)
        for bit in (1, 2, 4):
            sub_bit = (sub_b & bit) != 0
            lane_bit = (lane_b & bit) != 0
            from_up = pltpu.roll(pltpu.roll(cube, bit, 1), 128 - 16 * bit, 2)
            from_down = pltpu.roll(pltpu.roll(cube, 8 - bit, 1), 16 * bit, 2)
            cube = jnp.where(sub_bit == lane_bit, cube, jnp.where(sub_bit, from_up, from_down))
        top = 8 + 8 * (k % 2)
        for j in range(15):
            ipad[k // 2, top : top + 8, 128 * j : 128 * (j + 1)] = cube[j]

    image_halo = halo(ipad, 1)
    image_out[...] = ipad[:, 8:24, :]
    settle(s2buf, 127, 6, two_send)
    for copy in image_halo:
        copy.wait()
    ipad[:, 0:8, :] = ipad[:, 0:8, :] * keep_top
    ipad[:, 24:32, :] = ipad[:, 24:32, :] * keep_bottom

    def image_columns(j, carry):
        lanes = pl.ds(pl.multiple_of(128 * j, 128), 128)
        for ch in range(3):

            def terms(k):
                x = ipad[ch, 8 + k : 24 + k, lanes]
                return [x, x * x, x * tpad[ch, 8 + k : 24 + k, lanes]]

            found = down_columns(terms)
            for n in range(3):
                vert[3 * n + ch, :, lanes] = found[n]
        return carry

    lax.fori_loop(0, 15, image_columns, 0)
    along_rows(9, blur_i)

    def finish(j, carry):
        lanes = pl.ds(pl.multiple_of(128 * j, 128), 128)
        apart = jnp.zeros((16, 128), F32)
        alike = jnp.zeros((16, 128), F32)
        for ch in range(3):
            mx, sxx, sxy = [blur_i[3 * n + ch, :, lanes] for n in range(3)]
            my, syy = blur_t[ch, :, lanes], blur_t[3 + ch, :, lanes]
            mxx, myy, mxy = mx * mx, my * my, mx * my
            above_line = (2.0 * mxy + 0.0001) * (2.0 * (sxy - mxy) + 0.0009)
            below_line = (mxx + myy + 0.0001) * ((sxx - mxx) + (syy - myy) + 0.0009)
            alike = alike + above_line / below_line
            apart = apart + jnp.abs(ipad[ch, 8:24, lanes] - tpad[ch, 8:24, lanes])
        loss_out[:, lanes] = 0.8 * (apart * (1.0 / 3.0)) + 0.2 * (1.0 - alike * (1.0 / 3.0))
        return carry

    lax.fori_loop(0, 15, finish, 0)


def local(gauss_params, visible, cameras, tile_ids, tile_blocks, target):
    vmem = pl.BlockSpec(memory_space=pltpu.VMEM)
    hbm = pl.BlockSpec(memory_space=pl.ANY)
    dma = pltpu.SemaphoreType.DMA
    image, loss = pl.pallas_call(
        kernel,
        out_shape=(
            jax.ShapeDtypeStruct((3, 16, 1920), F32),
            jax.ShapeDtypeStruct((16, 1920), F32),
        ),
        in_specs=[hbm, hbm, pl.BlockSpec(memory_space=pltpu.SMEM), vmem, vmem, vmem],
        out_specs=(vmem, vmem),
        scratch_shapes=[
            pltpu.VMEM((59, NBP, 128), F32),
            pltpu.VMEM((4, NBP, 128), jnp.int32),
            pltpu.VMEM((8, 128), F32),
            pltpu.VMEM((256, 1, 128), jnp.int32),
            pltpu.VMEM((256, 1, 128), jnp.int32),
            pltpu.VMEM((128, 256), BF16),
            pltpu.VMEM((128, 256), BF16),
            pltpu.VMEM((NBP, 128), F32),
            pltpu.VMEM((9, NBP, 128), F32),
            pltpu.VMEM((2, 9, 128, 128), F32),
            pltpu.VMEM((8, 128, 128), F32),
            pltpu.VMEM((256, 8, 128), F32),
            pltpu.VMEM((256, 8, 128), F32),
            pltpu.VMEM((128, 8, 128), F32),
            pltpu.VMEM((128, 8, 128), F32),
            pltpu.VMEM((3, 32, 1920), F32),
            pltpu.VMEM((3, 32, 1920), F32),
            pltpu.VMEM((9, 16, 2048), F32),
            pltpu.VMEM((6, 16, 1920), F32),
            pltpu.VMEM((9, 16, 1920), F32),
            dma((2,)),
            dma,
            dma,
            dma((4,)),
            dma((4,)),
            dma,
            dma,
            dma,
            dma,
            dma,
        ],
        compiler_params=pltpu.CompilerParams(
            collective_id=0, has_side_effects=True, vmem_limit_bytes=48 << 20
        ),
    )(gauss_params, visible, cameras, tile_ids[0], tile_blocks[0, 0], target[0])
    return (image[None], loss[None])


def solution(mesh):
    return jax.shard_map(
        local,
        mesh=mesh,
        in_specs=(
            P(None, ("cell", "view")),
            P(None, ("cell", "view")),
            P(),
            P("cell", "view", None),
            P("cell", "view", None, None),
            P("view", None, "cell", None),
        ),
        out_specs=(P("view", None, "cell", None), P("view", "cell", None)),
        check_vma=False,
    )
```

time: 393 us -> 123 us (0.31); the launches traced: 387 us -> 123 us
  Pallas kernels: 0 us -> 114 us
  matrix products: 95.5 us -> 0 us
  local copies, waits for them, and re-layouts: 91.8 us -> 7.85 us
  other arithmetic: 79.8 us -> 0 us
  waiting for transfers between devices: 53.6 us -> 0 us
  starting transfers between devices: 51.1 us -> 0 us
  blocking collectives: 13.1 us -> 0 us
    pallas_call x0 -> x1, Pallas kernels: none -> 114 us  [local(): pl.pallas_call(kernel, out_shape=(jax.ShapeDtypeStruct((3, 16, 1920), F32...]
    dot_general x4 -> x0, matrix products: 95.5 us -> none  [the longest x2 55.3 us: blend_slot(): jnp.einsum('tpg,tcg->tcp', weights, features[:, 6:9], precision=lax.Preci...]
    all_to_all x4 -> x0, starting transfers between devices: 49.6 us -> none  [the longest x1 16.3 us: local(): lax.all_to_all(asks, 'cell', split_axis=0, concat_axis=0, tiled=True)]
    all_to_all x4 -> x0, waiting for transfers between devices: 42.6 us -> none  [the longest x1 29.6 us: local(): lax.all_to_all(served, 'cell', split_axis=0, concat_axis=0, tiled=True)]
    add x9 -> x0, other arithmetic: 42.5 us -> none  [the longest x1 19.2 us: blur(): sum((taps[number] * across[..., number:number + row_count, :] for number...]
    slice x10 -> x0, local copies, waits for them, and re-layouts: 33 us -> none  [the longest x3 28.5 us: project(): raw_params[:, 11 + 3 * number + channel]]
    reduce_sum x7 -> x0, other arithmetic: 19.5 us -> none  [the longest x1 17 us: blend_slot(): return (log_trans + jnp.sum(log_keep, axis=2), colour)]
    all_to_all x2 -> x0, blocking collectives: 13.1 us -> none  [the longest x1 8.24 us: local(): lax.all_to_all(lax.all_to_all(served, 'cell', split_axis=0, concat_axis=0...]
  transfers between devices with their start and end apart: 6 -> 0, of which waited for: 4 -> 0; matrix products, arithmetic and copies ran while one was open for 37% -> 0% of each run, Pallas kernels for 0% -> 0%
where the time goes in v1:
time: 123 us
  Pallas kernels  114 us (93%)
  local copies, waits for them, and re-layouts  7.85 us (6%)
    pallas_call x1, Pallas kernels, local(): pl.pallas_call(kernel, out_shape=(jax.ShapeDtypeStruct((3, 16, 1920), F32...  114 us
    unnamed x13, local copies, waits for them, and re-layouts  7.85 us

profile of v1, /device:TPU:1, one launch (start us, length us, event | category | flops | bytes accessed | tf_op | source)
XLA Modules:
  0.0 122.9 jit_solution(881479942431561038)
XLA Ops:
  0.6 0.8 copy.8
  1.4 0.0 copy-start
  1.4 2.4 %copy-done = f32[59,19200]{1,0:T(8,128)S(1)} copy-done((f32[59,19200]{1,0:T(8,128)S(1)}, f32[59,19200]{1,0:T(8,128)}, u32[]{:S(2)}) %copy-start) | copy-done | bytes 4531224
  3.8 0.0 copy-start.1
  3.8 1.0 copy-done.1
  4.8 0.0 copy-start.2
  4.8 1.0 copy-done.2
  5.8 0.0 copy-start.3
  5.8 0.7 copy-done.3
  6.4 0.0 copy-start.4
  6.4 0.7 copy-done.4
  7.1 114.4 %shard_map.77 = (f32[3,16,1920]{2,1,0:T(8,128)S(1)}, f32[16,1920]{1,0:T(8,128)S(1)}) custom-call(f32[59,19200]{1,0:T(8,128)S(1)} %copy-done, s32[4,19200]{1,0:T(4,128)S(1)} %copy-done.2, f32[4,15]{1,0:T(4,128)S(1)} %copy-done.3, s32[1,120]{1,0:T(1,128)S(1)} %bitcast.9, s32[120,2]{1,0:T(8,128)S(1)} %bitcast.7, f32[3,16,1920]{2,1,0:T(8,128)S(1)} %bitcast.6), custom_call_target="tpu_custom_call" | custom-call | tf_op jit(solution)/shard_map/pallas_call | solution.py:525
  121.5 0.7 copy.11
  122.2 0.6 copy.12
Async XLA Ops:
  1.4 2.4 %copy-start = (f32[59,19200]{1,0:T(8,128)S(1)}, f32[59,19200]{1,0:T(8,128)}, u32[]{:S(2)}) copy-start(f32[59,19200]{1,0:T(8,128)} %params.1) | copy-start | bytes 13593604
  3.8 1.0 copy-start.1
  4.8 1.0 copy-start.2
  5.8 0.7 copy-start.3
  6.4 0.7 copy-start.4

commit v2 on v1

--- a/solution.py
+++ b/solution.py
@@ -124,6 +124,18 @@
     ] + colours
 
 
+def steps(first, last, body):
+    def eight(i, carry):
+        for n in range(8):
+            body(first + 8 * i + n)
+        return carry
+
+    whole = (last - first) // 8
+    lax.fori_loop(0, whole, eight, 0)
+    for k in range(first + 8 * whole, last):
+        body(k)
+
+
 def kernel(
     params,
     visible,
@@ -135,25 +147,31 @@
     loss_out,
     par_s,
     vis_s,
-    tid_s,
+    tid_i,
+    blk_i,
+    list_s,
+    pick,
     req,
     rreq,
-    pick1,
-    pick2,
     view_s,
     feat,
     grid_f,
     px_s,
-    sbuf,
-    rbuf,
-    s2buf,
-    r2buf,
+    sbuf0,
+    sbuf1,
+    rbuf0,
+    rbuf1,
+    s2buf0,
+    s2buf1,
+    r2buf0,
+    r2buf1,
     tpad,
     ipad,
     vert,
     blur_t,
     blur_i,
     load_sem,
+    small_sem,
     req_send,
     req_recv,
     halo_send,
@@ -170,14 +188,21 @@
 
     barrier = pltpu.get_barrier_semaphore()
 
-    def greet(k, carry):
+    small = [
+        pltpu.make_async_copy(tile_ids, tid_i, small_sem.at[0]),
+        pltpu.make_async_copy(tile_blocks, blk_i, small_sem.at[1]),
+        pltpu.make_async_copy(target, tpad.at[:, pl.ds(8, 16), :], small_sem.at[2]),
+    ]
+    for copy in small:
+        copy.start()
+
+    def greet(k):
         cell = lax.rem(my_c + k, CELLS)
         pl.semaphore_signal(barrier, inc=1, device_id=(cell, my_v), device_id_type=MESH)
         pl.semaphore_signal(barrier, inc=1, device_id=(cell, 1 - my_v), device_id_type=MESH)
-        return carry
 
     pl.semaphore_signal(barrier, inc=1, device_id=(my_c, 1 - my_v), device_id_type=MESH)
-    lax.fori_loop(1, CELLS, greet, 0)
+    steps(1, CELLS, greet)
 
     par_s[:, NB:NBP, :] = jnp.zeros((59, NBP - NB, 128), F32)
     vis_s[:, NB:NBP, :] = jnp.zeros((4, NBP - NB, 128), jnp.int32)
@@ -190,20 +215,25 @@
 
     lax.fori_loop(0, NB, load, 0)
 
-    tid_s[...] = jnp.full((8, 128), -1.0, F32)
-    tid_s[0:1, 0:TILES] = tile_ids[...].astype(F32)
-    tid = jnp.transpose(jnp.broadcast_to(tid_s[0:1, :], (128, 128)))[0:TILES, 0:1].astype(jnp.int32)
+    list_s[...] = jnp.full((8, 128), -1.0, F32)
+    small[0].wait()
+    small[1].wait()
+    list_s[0:1, 0:TILES] = tid_i[...].astype(F32)
+    list_s[1:3, 0:TILES] = blk_i[...].astype(F32)
+    lists = jnp.transpose(list_s[...])[0:TILES].astype(jnp.int32)
+    tid = lists[:, 0:1]
     stripe = quotient(tid, TILES)
     column = tid - TILES * stripe
     lane2 = iota((TILES, 256), 1)
     hits = []
     local = []
     for entry in range(2):
-        block = tile_blocks[:, entry : entry + 1]
+        block = lists[:, 1 + entry : 2 + entry]
         owner = quotient(jnp.maximum(block, 0), NB)
         cell = owner // 2
         slot = (owner - 2 * cell) * CELLS + cell
-        hits.append((jnp.where(block >= 0, slot, -1) == lane2).astype(F32))
+        slot = jnp.where(block >= 0, slot, -1)
+        hits.append((slot == lane2).astype(F32))
         local.append((block - NB * owner + 1).astype(F32))
     by_stripe = (stripe == iota((TILES, 128), 1)).astype(F32)
     lb_row = jnp.sum(hits[0] * local[0] + hits[1] * local[1], axis=0, keepdims=True) - 1.0
@@ -217,14 +247,15 @@
         )
         req[lanes, 0, :] = jnp.transpose(text).astype(jnp.int32)
     stripe_hot = by_stripe.astype(BF16)
-    pick1[...] = dot00(stripe_hot, hits[0].astype(BF16)).astype(BF16)
-    pick2[...] = dot00(stripe_hot, hits[1].astype(BF16)).astype(BF16)
-    tpad[:, 8:24, :] = target[...]
+    for entry in range(2):
+        rows = slice(128 * entry, 128 * (entry + 1))
+        pick[rows, :] = dot00(stripe_hot, hits[entry].astype(BF16)).astype(BF16)
+    small[2].wait()
 
     pl.semaphore_wait(barrier, 2 * CELLS - 1)
 
     def exchange(src, dst, rows, send, recv, view, first):
-        def go(k, carry):
+        def go(k):
             cell = lax.rem(my_c + k, CELLS)
             pltpu.make_async_remote_copy(
                 src_ref=src.at[view * CELLS + cell, pl.ds(0, rows)],
@@ -234,9 +265,8 @@
                 device_id=(cell, view),
                 device_id_type=MESH,
             ).start()
-            return carry
-
-        lax.fori_loop(first, CELLS, go, 0)
+
+        steps(first, CELLS, go)
 
     def settle(ref, count, rows, sem):
         part = ref.at[pl.ds(0, count), pl.ds(0, rows)]
@@ -253,28 +283,19 @@
     above = lax.rem(my_c + CELLS - 1, CELLS)
     below = lax.rem(my_c + 1, CELLS)
 
-    def halo(buf, number):
-        up = pltpu.make_async_remote_copy(
-            src_ref=buf.at[:, pl.ds(8, 8), :],
-            dst_ref=buf.at[:, pl.ds(24, 8), :],
-            send_sem=halo_send.at[2 * number],
-            recv_sem=halo_recv.at[2 * number],
-            device_id=(above, my_v),
+    def halo(buf, number, way):
+        copy = pltpu.make_async_remote_copy(
+            src_ref=buf.at[:, pl.ds(8 + 8 * way, 8), :],
+            dst_ref=buf.at[:, pl.ds(24 - 24 * way, 8), :],
+            send_sem=halo_send.at[2 * number + way],
+            recv_sem=halo_recv.at[2 * number + way],
+            device_id=(below if way else above, my_v),
             device_id_type=MESH,
         )
-        down = pltpu.make_async_remote_copy(
-            src_ref=buf.at[:, pl.ds(16, 8), :],
-            dst_ref=buf.at[:, pl.ds(0, 8), :],
-            send_sem=halo_send.at[2 * number + 1],
-            recv_sem=halo_recv.at[2 * number + 1],
-            device_id=(below, my_v),
-            device_id_type=MESH,
-        )
-        up.start()
-        down.start()
-        return up, down
-
-    target_halo = halo(tpad, 0)
+        copy.start()
+        return copy
+
+    target_halo = [halo(tpad, 0, way) for way in range(2)]
     own(req.at[me_slot], rreq.at[me_slot])
     settle(rreq, 255, 1, req_recv)
 
@@ -331,8 +352,8 @@
 
     sub8 = iota((8, 128), 0).astype(F32)
 
-    def render(view):
-        for quarter in range(4):
+    def render(view, part, sbuf):
+        for quarter in (2 * part, 2 * part + 1):
 
             def blend(g, state):
                 state = list(state)
@@ -357,20 +378,23 @@
 
             zero = jnp.zeros((8, 128), F32)
             one = jnp.ones((8, 128), F32)
-            state = lax.fori_loop(0, 128, blend, (zero, zero, zero, one) * 8)
+            state = lax.fori_loop(0, 128, blend, (zero, zero, zero, one) * 8, unroll=4)
             for at in range(8):
                 start = 64 * (quarter % 2) + 8 * at
                 for k in range(4):
-                    px_s[2 * k + quarter // 2, start : start + 8, :] = state[4 * at + k]
+                    px_s[k, start : start + 8, :] = state[4 * at + k]
         rows = pl.ds(pl.multiple_of(view * CELLS, CELLS), CELLS)
-        for k in range(8):
+        for k in range(4):
             sbuf[rows, k, :] = jnp.transpose(px_s[k])
 
-    render(my_v)
-    exchange(sbuf, rbuf, 8, one_send, one_recv, my_v, 1)
-    own(sbuf.at[me_slot], rbuf.at[me_slot])
-    render(1 - my_v)
-    exchange(sbuf, rbuf, 8, one_send, one_recv, 1 - my_v, 0)
+    sent = [sbuf0, sbuf1]
+    got = [rbuf0, rbuf1]
+    for part in range(2):
+        render(my_v, part, sent[part])
+        exchange(sent[part], got[part], 4, one_send.at[part], one_recv.at[part], my_v, 1)
+        own(sent[part].at[me_slot], got[part].at[me_slot])
+        render(1 - my_v, part, sent[part])
+        exchange(sent[part], got[part], 4, one_send.at[part], one_recv.at[part], 1 - my_v, 0)
 
     taps = [0.0] * 6
     total = sum(2.718281828459045 ** (-(k * k) / 4.5) for k in range(-5, 6))
@@ -425,60 +449,63 @@
     along_rows(6, blur_t)
 
     settle(req, 255, 1, req_send)
-    settle(rbuf, 255, 8, one_recv)
-    hot1 = pick1[...]
-    hot2 = pick2[...]
-
-    def both(k):
-        parts = pieces(rbuf[:, k, :])
-        first = (dot10(hot1, parts[2]) + dot10(hot1, parts[1])) + dot10(hot1, parts[0])
-        if k >= 6:
-            return first, None
-        second = (dot10(hot2, parts[2]) + dot10(hot2, parts[1])) + dot10(hot2, parts[0])
-        return first, second
-
-    clear = [both(6)[0], both(7)[0]]
-    for k in range(6):
-        first, second = both(k)
-        s2buf[:, k, :] = first + clear[k % 2] * second
-
-    def exchange2(k, carry):
-        cell = lax.rem(my_c + k, CELLS)
-        pltpu.make_async_remote_copy(
-            src_ref=s2buf.at[cell, pl.ds(0, 6)],
-            dst_ref=r2buf.at[my_c, pl.ds(0, 6)],
-            send_sem=two_send,
-            recv_sem=two_recv,
-            device_id=(cell, my_v),
-            device_id_type=MESH,
-        ).start()
-        return carry
-
-    lax.fori_loop(1, CELLS, exchange2, 0)
-    own(s2buf.at[my_c], r2buf.at[my_c])
-    settle(sbuf, 255, 8, one_send)
-    settle(r2buf, 127, 6, two_recv)
+    sent2 = [s2buf0, s2buf1]
+    got2 = [r2buf0, r2buf1]
+
+    for part in range(2):
+        tiles, out, arrived = got[part], sent2[part], got2[part]
+        settle(tiles, 255, 4, one_recv.at[part])
+
+        hot = pick[...]
+        pairs = []
+        for k in (0, 2):
+            parts = pieces(jnp.concatenate([tiles[:, k, :], tiles[:, k + 1, :]], axis=1))
+            pairs.append((dot10(hot, parts[2]) + dot10(hot, parts[1])) + dot10(hot, parts[0]))
+        clear = pairs[1][0:128, 128:256]
+        for k in range(3):
+            pair, lanes = pairs[k // 2], slice(128 * (k % 2), 128 * (k % 2) + 128)
+            out[:, k, :] = pair[0:128, lanes] + clear * pair[128:256, lanes]
+
+        def send_tile(k):
+            cell = lax.rem(my_c + k, CELLS)
+            pltpu.make_async_remote_copy(
+                src_ref=out.at[cell, pl.ds(0, 3)],
+                dst_ref=arrived.at[my_c, pl.ds(0, 3)],
+                send_sem=two_send.at[part],
+                recv_sem=two_recv.at[part],
+                device_id=(cell, my_v),
+                device_id_type=MESH,
+            ).start()
+
+        steps(1, CELLS, send_tile)
+        own(out.at[my_c], arrived.at[my_c])
+    settle(sbuf0, 255, 4, one_send.at[0])
+    settle(sbuf1, 255, 4, one_send.at[1])
 
     hot_col = (iota((TILES, 128), 0) == cols_in).astype(BF16)
     sub_b = iota((15, 8, 128), 1)
     lane_b = iota((15, 8, 128), 2) // 16
-    for k in range(6):
-        parts = pieces(r2buf[:, k, :])
-        found = (dot10(hot_col, parts[2]) + dot10(hot_col, parts[1])) + dot10(hot_col, parts[0])
-        cube = found.reshape(15, 8, 128)
-        for bit in (1, 2, 4):
-            sub_bit = (sub_b & bit) != 0
-            lane_bit = (lane_b & bit) != 0
-            from_up = pltpu.roll(pltpu.roll(cube, bit, 1), 128 - 16 * bit, 2)
-            from_down = pltpu.roll(pltpu.roll(cube, 8 - bit, 1), 16 * bit, 2)
-            cube = jnp.where(sub_bit == lane_bit, cube, jnp.where(sub_bit, from_up, from_down))
-        top = 8 + 8 * (k % 2)
-        for j in range(15):
-            ipad[k // 2, top : top + 8, 128 * j : 128 * (j + 1)] = cube[j]
-
-    image_halo = halo(ipad, 1)
+
+    image_halo = []
+    for part in range(2):
+        settle(got2[part], 127, 3, two_recv.at[part])
+        for ch in range(3):
+            parts = pieces(got2[part][:, ch, :])
+            found = (dot10(hot_col, parts[2]) + dot10(hot_col, parts[1])) + dot10(hot_col, parts[0])
+            cube = found.reshape(15, 8, 128)
+            for bit in (1, 2, 4):
+                sub_bit = (sub_b & bit) != 0
+                lane_bit = (lane_b & bit) != 0
+                from_up = pltpu.roll(pltpu.roll(cube, bit, 1), 128 - 16 * bit, 2)
+                from_down = pltpu.roll(pltpu.roll(cube, 8 - bit, 1), 16 * bit, 2)
+                cube = jnp.where(sub_bit == lane_bit, cube, jnp.where(sub_bit, from_up, from_down))
+            for j in range(15):
+                ipad[ch, 8 + 8 * part : 16 + 8 * part, 128 * j : 128 * (j + 1)] = cube[j]
+        image_halo.append(halo(ipad, 1, part))
+
     image_out[...] = ipad[:, 8:24, :]
-    settle(s2buf, 127, 6, two_send)
+    for part in range(2):
+        settle(sent2[part], 127, 3, two_send.at[part])
     for copy in image_halo:
         copy.wait()
     ipad[:, 0:8, :] = ipad[:, 0:8, :] * keep_top
@@ -520,7 +547,7 @@
 
 def local(gauss_params, visible, cameras, tile_ids, tile_blocks, target):
     vmem = pl.BlockSpec(memory_space=pltpu.VMEM)
-    hbm = pl.BlockSpec(memory_space=pl.ANY)
+    hbm = pl.BlockSpec(memory_space=pltpu.HBM)
     dma = pltpu.SemaphoreType.DMA
     image, loss = pl.pallas_call(
         kernel,
@@ -528,44 +555,50 @@
             jax.ShapeDtypeStruct((3, 16, 1920), F32),
             jax.ShapeDtypeStruct((16, 1920), F32),
         ),
-        in_specs=[hbm, hbm, pl.BlockSpec(memory_space=pltpu.SMEM), vmem, vmem, vmem],
+        in_specs=[hbm, hbm, pl.BlockSpec(memory_space=pltpu.SMEM), hbm, hbm, hbm],
         out_specs=(vmem, vmem),
         scratch_shapes=[
             pltpu.VMEM((59, NBP, 128), F32),
             pltpu.VMEM((4, NBP, 128), jnp.int32),
+            pltpu.VMEM((1, TILES), jnp.int32),
+            pltpu.VMEM((2, TILES), jnp.int32),
             pltpu.VMEM((8, 128), F32),
+            pltpu.VMEM((256, 256), BF16),
             pltpu.VMEM((256, 1, 128), jnp.int32),
             pltpu.VMEM((256, 1, 128), jnp.int32),
-            pltpu.VMEM((128, 256), BF16),
-            pltpu.VMEM((128, 256), BF16),
             pltpu.VMEM((NBP, 128), F32),
             pltpu.VMEM((9, NBP, 128), F32),
             pltpu.VMEM((2, 9, 128, 128), F32),
-            pltpu.VMEM((8, 128, 128), F32),
-            pltpu.VMEM((256, 8, 128), F32),
-            pltpu.VMEM((256, 8, 128), F32),
-            pltpu.VMEM((128, 8, 128), F32),
-            pltpu.VMEM((128, 8, 128), F32),
+            pltpu.VMEM((4, 128, 128), F32),
+            pltpu.VMEM((256, 4, 128), F32),
+            pltpu.VMEM((256, 4, 128), F32),
+            pltpu.VMEM((256, 4, 128), F32),
+            pltpu.VMEM((256, 4, 128), F32),
+            pltpu.VMEM((128, 4, 128), F32),
+            pltpu.VMEM((128, 4, 128), F32),
+            pltpu.VMEM((128, 4, 128), F32),
+            pltpu.VMEM((128, 4, 128), F32),
             pltpu.VMEM((3, 32, 1920), F32),
             pltpu.VMEM((3, 32, 1920), F32),
             pltpu.VMEM((9, 16, 2048), F32),
             pltpu.VMEM((6, 16, 1920), F32),
             pltpu.VMEM((9, 16, 1920), F32),
             dma((2,)),
+            dma((4,)),
             dma,
             dma,
             dma((4,)),
             dma((4,)),
-            dma,
-            dma,
-            dma,
-            dma,
+            dma((2,)),
+            dma((2,)),
+            dma((2,)),
+            dma((2,)),
             dma,
         ],
         compiler_params=pltpu.CompilerParams(
-            collective_id=0, has_side_effects=True, vmem_limit_bytes=48 << 20
+            collective_id=0, has_side_effects=True, vmem_limit_bytes=60 << 20
         ),
-    )(gauss_params, visible, cameras, tile_ids[0], tile_blocks[0, 0], target[0])
+    )(gauss_params, visible, cameras, tile_ids[0], tile_blocks[0, 0].T, target[0])
     return (image[None], loss[None])
 
 

time: 123 us -> 89.7 us (0.73)
  Pallas kernels: 114 us -> 85.6 us
  local copies, waits for them, and re-layouts: 7.85 us -> 3.31 us
    pallas_call x1, Pallas kernels: 114 us -> 85.6 us  [local(): pl.pallas_call(kernel, out_shape=(jax.ShapeDtypeStruct((3, 16, 1920), F32...]
    unnamed x13 -> x2, local copies, waits for them, and re-layouts: 7.85 us -> 3.31 us
where the time goes in v2:
time: 89.7 us; the launch traced here: 89.5 us
  Pallas kernels  85.6 us (95%)
  local copies, waits for them, and re-layouts  3.31 us (4%)
    pallas_call x1, Pallas kernels, local(): pl.pallas_call(kernel, out_shape=(jax.ShapeDtypeStruct((3, 16, 1920), F32...  85.6 us
    unnamed x2, local copies, waits for them, and re-layouts  3.31 us

profile of v2, /device:TPU:1, one launch (start us, length us, event | category | flops | bytes accessed | tf_op | source)
XLA Modules:
  0.0 89.5 jit_solution(3811961481271062094)
XLA Ops:
  0.6 85.6 %shard_map.77 = (f32[3,16,1920]{2,1,0:T(8,128)}, f32[16,1920]{1,0:T(8,128)}) custom-call(f32[59,19200]{1,0:T(8,128)} %params.1, s32[4,19200]{1,0:T(4,128)} %visible.1, f32[4,15]{1,0:T(4,128)} %cam.1, s32[1,120]{1,0:T(1,128)} %bitcast.11, s32[2,120]{1,0:T(2,128)} %bitcast.10, f32[3,16,1920]{2,1,0:T(8,128)} %bitcast.8), custom_call_target="tpu_custom_call" | custom-call | tf_op jit(solution)/shard_map/pallas_call | solution.py:552
  86.2 1.7 %copy.10 = f32[1,3,16,1920]{3,2,1,0:T(8,128)} copy(f32[1,3,16,1920]{3,2,1,0:T(8,128)} %bitcast.7) | data formatting | bytes 737280
  88.0 1.6 %copy.11 = f32[1,16,1920]{2,1,0:T(8,128)} copy(f32[1,16,1920]{2,1,0:T(8,128)} %bitcast.9) | data formatting | bytes 245760

commit v3 on v2

--- a/solution.py
+++ b/solution.py
@@ -167,6 +167,8 @@
     r2buf1,
     tpad,
     ipad,
+    edge_out,
+    edge_in,
     vert,
     blur_t,
     blur_i,
@@ -197,7 +199,7 @@
         copy.start()
 
     def greet(k):
-        cell = lax.rem(my_c + k, CELLS)
+        cell = (my_c + k) & (CELLS - 1)
         pl.semaphore_signal(barrier, inc=1, device_id=(cell, my_v), device_id_type=MESH)
         pl.semaphore_signal(barrier, inc=1, device_id=(cell, 1 - my_v), device_id_type=MESH)
 
@@ -256,7 +258,7 @@
 
     def exchange(src, dst, rows, send, recv, view, first):
         def go(k):
-            cell = lax.rem(my_c + k, CELLS)
+            cell = (my_c + k) & (CELLS - 1)
             pltpu.make_async_remote_copy(
                 src_ref=src.at[view * CELLS + cell, pl.ds(0, rows)],
                 dst_ref=dst.at[me_slot, pl.ds(0, rows)],
@@ -284,9 +286,14 @@
     below = lax.rem(my_c + 1, CELLS)
 
     def halo(buf, number, way):
+        if way:
+            edge_out[number, :, 0:5, :] = buf[:, 19:24, :]
+            src, dst = edge_out.at[number, :, pl.ds(0, 5), :], edge_in.at[number, :, pl.ds(0, 5), :]
+        else:
+            src, dst = buf.at[:, pl.ds(8, 5), :], buf.at[:, pl.ds(24, 5), :]
         copy = pltpu.make_async_remote_copy(
-            src_ref=buf.at[:, pl.ds(8 + 8 * way, 8), :],
-            dst_ref=buf.at[:, pl.ds(24 - 24 * way, 8), :],
+            src_ref=src,
+            dst_ref=dst,
             send_sem=halo_send.at[2 * number + way],
             recv_sem=halo_recv.at[2 * number + way],
             device_id=(below if way else above, my_v),
@@ -423,12 +430,12 @@
             out[plane, rows, :] = acc[:, 0:1920]
             return carry
 
-        lax.fori_loop(0, 2 * count, go, 0)
+        lax.fori_loop(0, 2 * count, go, 0, unroll=6)
 
     for copy in target_halo:
         copy.wait()
-    tpad[:, 0:8, :] = tpad[:, 0:8, :] * keep_top
-    tpad[:, 24:32, :] = tpad[:, 24:32, :] * keep_bottom
+    tpad[:, 3:8, :] = edge_in[0, :, 0:5, :] * keep_top
+    tpad[:, 24:29, :] = tpad[:, 24:29, :] * keep_bottom
     for plane in range(9):
         vert[plane, :, 1920:2048] = jnp.zeros((16, 128), F32)
 
@@ -467,7 +474,7 @@
             out[:, k, :] = pair[0:128, lanes] + clear * pair[128:256, lanes]
 
         def send_tile(k):
-            cell = lax.rem(my_c + k, CELLS)
+            cell = (my_c + k) & (CELLS - 1)
             pltpu.make_async_remote_copy(
                 src_ref=out.at[cell, pl.ds(0, 3)],
                 dst_ref=arrived.at[my_c, pl.ds(0, 3)],
@@ -503,13 +510,14 @@
                 ipad[ch, 8 + 8 * part : 16 + 8 * part, 128 * j : 128 * (j + 1)] = cube[j]
         image_halo.append(halo(ipad, 1, part))
 
-    image_out[...] = ipad[:, 8:24, :]
+    image_copy = pltpu.make_async_copy(ipad.at[:, pl.ds(8, 16), :], image_out, small_sem.at[3])
+    image_copy.start()
     for part in range(2):
         settle(sent2[part], 127, 3, two_send.at[part])
     for copy in image_halo:
         copy.wait()
-    ipad[:, 0:8, :] = ipad[:, 0:8, :] * keep_top
-    ipad[:, 24:32, :] = ipad[:, 24:32, :] * keep_bottom
+    ipad[:, 3:8, :] = edge_in[1, :, 0:5, :] * keep_top
+    ipad[:, 24:29, :] = ipad[:, 24:29, :] * keep_bottom
 
     def image_columns(j, carry):
         lanes = pl.ds(pl.multiple_of(128 * j, 128), 128)
@@ -543,6 +551,7 @@
         return carry
 
     lax.fori_loop(0, 15, finish, 0)
+    image_copy.wait()
 
 
 def local(gauss_params, visible, cameras, tile_ids, tile_blocks, target):
@@ -556,7 +565,7 @@
             jax.ShapeDtypeStruct((16, 1920), F32),
         ),
         in_specs=[hbm, hbm, pl.BlockSpec(memory_space=pltpu.SMEM), hbm, hbm, hbm],
-        out_specs=(vmem, vmem),
+        out_specs=(hbm, vmem),
         scratch_shapes=[
             pltpu.VMEM((59, NBP, 128), F32),
             pltpu.VMEM((4, NBP, 128), jnp.int32),
@@ -580,6 +589,8 @@
             pltpu.VMEM((128, 4, 128), F32),
             pltpu.VMEM((3, 32, 1920), F32),
             pltpu.VMEM((3, 32, 1920), F32),
+            pltpu.VMEM((2, 3, 8, 1920), F32),
+            pltpu.VMEM((2, 3, 8, 1920), F32),
             pltpu.VMEM((9, 16, 2048), F32),
             pltpu.VMEM((6, 16, 1920), F32),
             pltpu.VMEM((9, 16, 1920), F32),

time: 89.7 us -> 87 us (0.970)
  Pallas kernels: 85.6 us -> 82.9 us
    pallas_call x1, Pallas kernels: 85.6 us -> 82.9 us  [local(): pl.pallas_call(kernel, out_shape=(jax.ShapeDtypeStruct((3, 16, 1920), F32...]
where the time goes in v3:
time: 87 us; the launch traced here: 86.9 us
  Pallas kernels  82.9 us (95%)
  local copies, waits for them, and re-layouts  3.31 us (4%)
    pallas_call x1, Pallas kernels, local(): pl.pallas_call(kernel, out_shape=(jax.ShapeDtypeStruct((3, 16, 1920), F32...  82.9 us
    unnamed x2, local copies, waits for them, and re-layouts  3.31 us

profile of v3, /device:TPU:1, one launch (start us, length us, event | category | flops | bytes accessed | tf_op | source)
XLA Modules:
  0.0 86.9 jit_solution(11540688377919715041)
XLA Ops:
  0.6 82.9 %shard_map.77 = (f32[3,16,1920]{2,1,0:T(8,128)}, f32[16,1920]{1,0:T(8,128)}) custom-call(f32[59,19200]{1,0:T(8,128)} %params.1, s32[4,19200]{1,0:T(4,128)} %visible.1, f32[4,15]{1,0:T(4,128)} %cam.1, s32[1,120]{1,0:T(1,128)} %bitcast.11, s32[2,120]{1,0:T(2,128)} %bitcast.10, f32[3,16,1920]{2,1,0:T(8,128)} %bitcast.8), custom_call_target="tpu_custom_call" | custom-call | tf_op jit(solution)/shard_map/pallas_call | solution.py:561
  83.6 1.7 %copy.10 = f32[1,3,16,1920]{3,2,1,0:T(8,128)} copy(f32[1,3,16,1920]{3,2,1,0:T(8,128)} %bitcast.7) | data formatting | bytes 737280
  85.3 1.6 %copy.11 = f32[1,16,1920]{2,1,0:T(8,128)} copy(f32[1,16,1920]{2,1,0:T(8,128)} %bitcast.9) | data formatting | bytes 245760

commit v4 on v3

--- a/solution.py
+++ b/solution.py
@@ -124,16 +124,21 @@
     ] + colours
 
 
-def steps(first, last, body):
+def cells_in_turn(my_c, own, body):
+    order = (4, 3, 5, 2, 6, 1, 7, 0)
+
     def eight(i, carry):
-        for n in range(8):
-            body(first + 8 * i + n)
+        place = (my_c + i + 1) & 15
+        for step in order:
+            body(((my_c + 16 * step) & (CELLS - 16)) + place)
         return carry
 
-    whole = (last - first) // 8
-    lax.fori_loop(0, whole, eight, 0)
-    for k in range(first + 8 * whole, last):
-        body(k)
+    lax.fori_loop(0, 15, eight, 0)
+    place = my_c & 15
+    for step in order[:7]:
+        body(((my_c + 16 * step) & (CELLS - 16)) + place)
+    if not own:
+        body(my_c)
 
 
 def kernel(
@@ -182,7 +187,6 @@
     one_recv,
     two_send,
     two_recv,
-    own_sem,
 ):
     my_c = lax.axis_index("cell")
     my_v = lax.axis_index("view")
@@ -193,19 +197,20 @@
     small = [
         pltpu.make_async_copy(tile_ids, tid_i, small_sem.at[0]),
         pltpu.make_async_copy(tile_blocks, blk_i, small_sem.at[1]),
-        pltpu.make_async_copy(target, tpad.at[:, pl.ds(8, 16), :], small_sem.at[2]),
+        pltpu.make_async_copy(target, tpad.at[:, pl.ds(8, 16), pl.ds(0, 1920)], small_sem.at[2]),
     ]
     for copy in small:
         copy.start()
 
-    def greet(k):
-        cell = (my_c + k) & (CELLS - 1)
+    def greet(cell):
         pl.semaphore_signal(barrier, inc=1, device_id=(cell, my_v), device_id_type=MESH)
         pl.semaphore_signal(barrier, inc=1, device_id=(cell, 1 - my_v), device_id_type=MESH)
 
     pl.semaphore_signal(barrier, inc=1, device_id=(my_c, 1 - my_v), device_id_type=MESH)
-    steps(1, CELLS, greet)
-
+    cells_in_turn(my_c, True, greet)
+
+    tpad[:, :, 1920:2048] = jnp.zeros((3, 32, 128), F32)
+    ipad[:, :, 1920:2048] = jnp.zeros((3, 32, 128), F32)
     par_s[:, NB:NBP, :] = jnp.zeros((59, NBP - NB, 128), F32)
     vis_s[:, NB:NBP, :] = jnp.zeros((4, NBP - NB, 128), jnp.int32)
 
@@ -257,9 +262,8 @@
     pl.semaphore_wait(barrier, 2 * CELLS - 1)
 
     def exchange(src, dst, rows, send, recv, view, first):
-        def go(k):
-            cell = (my_c + k) & (CELLS - 1)
-            pltpu.make_async_remote_copy(
+        def go(cell):
+                pltpu.make_async_remote_copy(
                 src_ref=src.at[view * CELLS + cell, pl.ds(0, rows)],
                 dst_ref=dst.at[me_slot, pl.ds(0, rows)],
                 send_sem=send,
@@ -268,17 +272,12 @@
                 device_id_type=MESH,
             ).start()
 
-        steps(first, CELLS, go)
+        cells_in_turn(my_c, first == 1, go)
 
     def settle(ref, count, rows, sem):
         part = ref.at[pl.ds(0, count), pl.ds(0, rows)]
         pltpu.make_async_copy(part, part, sem).wait()
 
-    def own(src, dst):
-        copy = pltpu.make_async_copy(src, dst, own_sem)
-        copy.start()
-        copy.wait()
-
     exchange(req, rreq, 1, req_send, req_recv, my_v, 1)
     exchange(req, rreq, 1, req_send, req_recv, 1 - my_v, 0)
 
@@ -287,10 +286,11 @@
 
     def halo(buf, number, way):
         if way:
-            edge_out[number, :, 0:5, :] = buf[:, 19:24, :]
+            edge_out[number, :, 0:5, :] = buf[:, 19:24, 0:1920]
             src, dst = edge_out.at[number, :, pl.ds(0, 5), :], edge_in.at[number, :, pl.ds(0, 5), :]
         else:
-            src, dst = buf.at[:, pl.ds(8, 5), :], buf.at[:, pl.ds(24, 5), :]
+            lanes = pl.ds(0, 1920)
+            src, dst = buf.at[:, pl.ds(8, 5), lanes], buf.at[:, pl.ds(24, 5), lanes]
         copy = pltpu.make_async_remote_copy(
             src_ref=src,
             dst_ref=dst,
@@ -303,7 +303,7 @@
         return copy
 
     target_halo = [halo(tpad, 0, way) for way in range(2)]
-    own(req.at[me_slot], rreq.at[me_slot])
+    rreq[me_slot] = req[me_slot]
     settle(rreq, 255, 1, req_recv)
 
     asked = rreq[:, 0, :].astype(F32)
@@ -370,12 +370,20 @@
                 dx = [sub8 - row[0], (sub8 + 8.0) - row[0]]
                 lead = [row[2] * d * d + row[5] for d in dx]
                 cross = [row[3] * d for d in dx]
+                dy = 4.0 * quarter - row[1]
+                bend = row[4] * dy
+                slope = (bend + bend) + row[4]
+                curve = row[4] + row[4]
+                power = [lead[half] + dy * (cross[half] + bend) for half in range(2)]
+                rise = [cross[half] + slope for half in range(2)]
                 for line in range(4):
-                    dy = (4.0 * quarter + line) - row[1]
-                    bend = row[4] * dy
                     for half in range(2):
                         at = 4 * (2 * line + half)
-                        alpha = jnp.exp2(lead[half] + dy * (cross[half] + bend))
+                        alpha = jnp.exp2(power[half])
+                        if line < 3:
+                            power[half] = power[half] + rise[half]
+                        if line < 2:
+                            rise[half] = rise[half] + curve
                         weight = alpha * state[at + 3]
                         state[at] = state[at] + weight * row[6]
                         state[at + 1] = state[at + 1] + weight * row[7]
@@ -399,7 +407,7 @@
     for part in range(2):
         render(my_v, part, sent[part])
         exchange(sent[part], got[part], 4, one_send.at[part], one_recv.at[part], my_v, 1)
-        own(sent[part].at[me_slot], got[part].at[me_slot])
+        got[part][me_slot] = sent[part][me_slot]
         render(1 - my_v, part, sent[part])
         exchange(sent[part], got[part], 4, one_send.at[part], one_recv.at[part], 1 - my_v, 0)
 
@@ -419,25 +427,33 @@
             totals = [t + taps[k] * (a + b) for t, a, b in zip(totals, lower, upper)]
         return totals
 
-    def along_rows(count, out):
-        def go(i, carry):
-            plane = i // 2
-            rows = pl.ds(pl.multiple_of(8 * (i % 2), 8), 8)
-            x = vert[plane, rows, :]
-            acc = taps[0] * x
-            for k in range(1, 6):
-                acc = acc + taps[k] * (pltpu.roll(x, k, 1) + pltpu.roll(x, 2048 - k, 1))
-            out[plane, rows, :] = acc[:, 0:1920]
+    def spread(x):
+        acc = taps[0] * x
+        for k in range(1, 6):
+            acc = acc + taps[k] * (pltpu.roll(x, k, 1) + pltpu.roll(x, 2048 - k, 1))
+        return acc[:, 0:1920]
+
+    def along_rows(i, carry):
+        rows = pl.ds(pl.multiple_of(8 * (i % 2), 8), 8)
+        blur_t[i // 2, rows, :] = spread(vert[i // 2, rows, :])
+        return carry
+
+    def image_rows(group):
+        rows = slice(8 * group, 8 * group + 8)
+
+        def go(ch, carry):
+            x = ipad[ch, rows, :]
+            for n, plane in enumerate((x, x * x, x * tpad[ch, rows, :])):
+                blur_i[3 * n + ch, rows, :] = spread(plane)
             return carry
 
-        lax.fori_loop(0, 2 * count, go, 0, unroll=6)
+        lax.fori_loop(0, 3, go, 0, unroll=3)
 
     for copy in target_halo:
         copy.wait()
-    tpad[:, 3:8, :] = edge_in[0, :, 0:5, :] * keep_top
-    tpad[:, 24:29, :] = tpad[:, 24:29, :] * keep_bottom
-    for plane in range(9):
-        vert[plane, :, 1920:2048] = jnp.zeros((16, 128), F32)
+    tpad[:, 3:8, 0:1920] = edge_in[0, :, 0:5, :] * keep_top
+    tpad[:, 24:29, 0:1920] = tpad[:, 24:29, 0:1920] * keep_bottom
+    vert[:, :, 1920:2048] = jnp.zeros((6, 16, 128), F32)
 
     def target_columns(j, carry):
         lanes = pl.ds(pl.multiple_of(128 * j, 128), 128)
@@ -453,7 +469,7 @@
         return carry
 
     lax.fori_loop(0, 15, target_columns, 0)
-    along_rows(6, blur_t)
+    lax.fori_loop(0, 12, along_rows, 0, unroll=6)
 
     settle(req, 255, 1, req_send)
     sent2 = [s2buf0, s2buf1]
@@ -473,9 +489,8 @@
             pair, lanes = pairs[k // 2], slice(128 * (k % 2), 128 * (k % 2) + 128)
             out[:, k, :] = pair[0:128, lanes] + clear * pair[128:256, lanes]
 
-        def send_tile(k):
-            cell = (my_c + k) & (CELLS - 1)
-            pltpu.make_async_remote_copy(
+        def send_tile(cell):
+                pltpu.make_async_remote_copy(
                 src_ref=out.at[cell, pl.ds(0, 3)],
                 dst_ref=arrived.at[my_c, pl.ds(0, 3)],
                 send_sem=two_send.at[part],
@@ -484,8 +499,8 @@
                 device_id_type=MESH,
             ).start()
 
-        steps(1, CELLS, send_tile)
-        own(out.at[my_c], arrived.at[my_c])
+        cells_in_turn(my_c, True, send_tile)
+        arrived[my_c] = out[my_c]
     settle(sbuf0, 255, 4, one_send.at[0])
     settle(sbuf1, 255, 4, one_send.at[1])
 
@@ -509,38 +524,32 @@
             for j in range(15):
                 ipad[ch, 8 + 8 * part : 16 + 8 * part, 128 * j : 128 * (j + 1)] = cube[j]
         image_halo.append(halo(ipad, 1, part))
-
-    image_copy = pltpu.make_async_copy(ipad.at[:, pl.ds(8, 16), :], image_out, small_sem.at[3])
+        if part == 0:
+            image_rows(1)
+
+    inner = ipad.at[:, pl.ds(8, 16), pl.ds(0, 1920)]
+    image_copy = pltpu.make_async_copy(inner, image_out, small_sem.at[3])
     image_copy.start()
+    image_rows(2)
+    image_halo[0].wait()
+    ipad[:, 24:29, 0:1920] = ipad[:, 24:29, 0:1920] * keep_bottom
+    image_rows(3)
     for part in range(2):
         settle(sent2[part], 127, 3, two_send.at[part])
-    for copy in image_halo:
-        copy.wait()
-    ipad[:, 3:8, :] = edge_in[1, :, 0:5, :] * keep_top
-    ipad[:, 24:29, :] = ipad[:, 24:29, :] * keep_bottom
-
-    def image_columns(j, carry):
-        lanes = pl.ds(pl.multiple_of(128 * j, 128), 128)
-        for ch in range(3):
-
-            def terms(k):
-                x = ipad[ch, 8 + k : 24 + k, lanes]
-                return [x, x * x, x * tpad[ch, 8 + k : 24 + k, lanes]]
-
-            found = down_columns(terms)
-            for n in range(3):
-                vert[3 * n + ch, :, lanes] = found[n]
-        return carry
-
-    lax.fori_loop(0, 15, image_columns, 0)
-    along_rows(9, blur_i)
+    image_halo[1].wait()
+    ipad[:, 3:8, 0:1920] = edge_in[1, :, 0:5, :] * keep_top
+    image_rows(0)
 
     def finish(j, carry):
         lanes = pl.ds(pl.multiple_of(128 * j, 128), 128)
         apart = jnp.zeros((16, 128), F32)
         alike = jnp.zeros((16, 128), F32)
         for ch in range(3):
-            mx, sxx, sxy = [blur_i[3 * n + ch, :, lanes] for n in range(3)]
+
+            def terms(k):
+                return [blur_i[3 * n + ch, 8 + k : 24 + k, lanes] for n in range(3)]
+
+            mx, sxx, sxy = down_columns(terms)
             my, syy = blur_t[ch, :, lanes], blur_t[3 + ch, :, lanes]
             mxx, myy, mxy = mx * mx, my * my, mx * my
             above_line = (2.0 * mxy + 0.0001) * (2.0 * (sxy - mxy) + 0.0009)
@@ -587,13 +596,13 @@
             pltpu.VMEM((128, 4, 128), F32),
             pltpu.VMEM((128, 4, 128), F32),
             pltpu.VMEM((128, 4, 128), F32),
-            pltpu.VMEM((3, 32, 1920), F32),
-            pltpu.VMEM((3, 32, 1920), F32),
+            pltpu.VMEM((3, 32, 2048), F32),
+            pltpu.VMEM((3, 32, 2048), F32),
             pltpu.VMEM((2, 3, 8, 1920), F32),
             pltpu.VMEM((2, 3, 8, 1920), F32),
-            pltpu.VMEM((9, 16, 2048), F32),
+            pltpu.VMEM((6, 16, 2048), F32),
             pltpu.VMEM((6, 16, 1920), F32),
-            pltpu.VMEM((9, 16, 1920), F32),
+            pltpu.VMEM((9, 32, 1920), F32),
             dma((2,)),
             dma((4,)),
             dma,
@@ -604,7 +613,6 @@
             dma((2,)),
             dma((2,)),
             dma((2,)),
-            dma,
         ],
         compiler_params=pltpu.CompilerParams(
             collective_id=0, has_side_effects=True, vmem_limit_bytes=60 << 20

time: 87 us -> 82.4 us (0.947)
  Pallas kernels: 82.9 us -> 78.3 us
    pallas_call x1, Pallas kernels: 82.9 us -> 78.3 us  [local(): pl.pallas_call(kernel, out_shape=(jax.ShapeDtypeStruct((3, 16, 1920), F32...]
where the time goes in v4:
time: 82.4 us; the launch traced here: 82.2 us
  Pallas kernels  78.3 us (95%)
  local copies, waits for them, and re-layouts  3.31 us (4%)
    pallas_call x1, Pallas kernels, local(): pl.pallas_call(kernel, out_shape=(jax.ShapeDtypeStruct((3, 16, 1920), F32...  78.3 us
    unnamed x2, local copies, waits for them, and re-layouts  3.31 us

profile of v4, /device:TPU:1, one launch (start us, length us, event | category | flops | bytes accessed | tf_op | source)
XLA Modules:
  0.0 82.2 jit_solution(8407713556460817378)
XLA Ops:
  0.6 78.3 %shard_map.77 = (f32[3,16,1920]{2,1,0:T(8,128)}, f32[16,1920]{1,0:T(8,128)}) custom-call(f32[59,19200]{1,0:T(8,128)} %params.1, s32[4,19200]{1,0:T(4,128)} %visible.1, f32[4,15]{1,0:T(4,128)} %cam.1, s32[1,120]{1,0:T(1,128)} %bitcast.11, s32[2,120]{1,0:T(2,128)} %bitcast.10, f32[3,16,1920]{2,1,0:T(8,128)} %bitcast.8), custom_call_target="tpu_custom_call" | custom-call | tf_op jit(solution)/shard_map/pallas_call | solution.py:570
  78.9 1.7 %copy.10 = f32[1,3,16,1920]{3,2,1,0:T(8,128)} copy(f32[1,3,16,1920]{3,2,1,0:T(8,128)} %bitcast.7) | data formatting | bytes 737280
  80.7 1.6 %copy.11 = f32[1,16,1920]{2,1,0:T(8,128)} copy(f32[1,16,1920]{2,1,0:T(8,128)} %bitcast.9) | data formatting | bytes 245760
